TPU v7x, 32 devices: a whole 2x2x4 slice. The times are simulated.
32 devices in a mesh: grp: 4 (over y, x), blk: 8 (over z, core).
Axes of the slice: x: 2, y: 2, z: 4, core: 2. Of those that a mesh axis runs over, the one named last changes fastest.
Arguments:
- source_emb: bfloat16 [6144, 768], P('blk'), may hold values from -32 to 32
- target_emb: bfloat16 [6144, 768], P(('grp', 'blk')), may hold values from -16 to 16
- hard_pool: bfloat16 [6144, 768], P(('grp', 'blk')), may hold values from -16 to 16
- hard_index: int32 [6144], P('blk'), may hold values from 0 to 6143, as said below
- language: int32 [6144], P('blk'), may hold values from 0 to 108
- margin: float32 [109], replicated, may hold values from 0.5 to 3
Outputs:
- row_loss: float32 [6144], P('blk')
- source_grad: float32 [6144, 768], P('blk')
- target_grad: float32 [6144, 768], P(('grp', 'blk'))
- pool_grad: float32 [6144, 768], P(('grp', 'blk'))
Inputs may be any that keep to these rules, and one draw needn't show every extreme that they name: `hard_index`: each entry is a row of hard_pool; an entry's owner is its value // 192. Within each aligned block of 192 entries no owner is named more than 12 times, and one owner, the same for all blocks, is named exactly 12 times in every block.
All inputs are finite; a program needn't handle non-finite values.
Results may differ from a plain program's by a relative error of at most 0.0025.
Values may be sent and summed in bfloat16 or wider, within the bound.
A program may use at most 64 MiB of HBM per device.

v0:
```python
import jax
import jax.numpy as jnp
from jax import lax
from jax.sharding import PartitionSpec as P

neg_fill = -1e30


def shifted(block, axis, distance):
    devices = range(lax.axis_size(axis))
    route = [((i - distance) % len(devices), i) for i in devices]
    return lax.ppermute(block, axis, route)


def merged(value, axis, join):
    pieces = jax.tree.map(lambda part: lax.all_gather(part, axis), value)
    head = jax.tree.map(lambda part: part[0], pieces)
    tail = jax.tree.map(lambda part: part[1:], pieces)
    so_far, _ = lax.scan(lambda so_far, piece: (join(so_far, piece), None), head, tail)
    return so_far


def combine(earlier, later):
    row_top = jnp.maximum(earlier[0], later[0])
    row_total = earlier[1] * jnp.exp(earlier[0] - row_top) + later[1] * jnp.exp(later[0] - row_top)
    return (row_top, row_total, earlier[2] + later[2])


def serve_rows(hard_pool, wanted):
    is_valid = wanted >= 0
    picked = jnp.take(hard_pool, jnp.maximum(wanted, 0), axis=0)
    return jnp.where(is_valid[..., None], picked, jnp.zeros_like(picked))


def shards(source_emb, target_emb, hard_pool, hard_index, language, margin):
    row_count = source_emb.shape[0]
    width = source_emb.shape[1]
    tgt_rows = target_emb.shape[0]
    blk_count = lax.axis_size("blk")
    grp_count = lax.axis_size("grp")
    owner_count = blk_count * grp_count
    slot_cap = max(2, (2 * tgt_rows + owner_count - 1) // owner_count)
    blk_index = lax.axis_index("blk")
    grp_index = lax.axis_index("grp")
    row_ids = blk_index * row_count + jnp.arange(row_count, dtype=jnp.int32)
    lang_match = language[:, None] == jnp.arange(margin.shape[0], dtype=jnp.int32)[None, :]
    margin_row = jnp.sum(jnp.where(lang_match, margin[None, :], 0.0), axis=1)
    column = jnp.arange(tgt_rows, dtype=jnp.int32)

    def global_cols(step_index):
        col_back = (
            grp_index * blk_count + (blk_index - step_index) % blk_count
        ) * tgt_rows + column
        return col_back

    def adjusted_scores(tgt_block, step_index):
        scores = jnp.einsum("rd,td->rt", source_emb, tgt_block, preferred_element_type=jnp.float32)
        positive = row_ids[:, None] == global_cols(step_index)[None, :]
        return (scores - jnp.where(positive, margin_row[:, None], 0.0), positive)

    own_start = grp_index * tgt_rows
    own_index = lax.dynamic_slice_in_dim(hard_index, own_start, tgt_rows, 0)
    own_source = lax.dynamic_slice_in_dim(source_emb, own_start, tgt_rows, 0)
    owner_index = own_index // tgt_rows
    pool_row = own_index % tgt_rows
    position = jnp.arange(tgt_rows, dtype=jnp.int32)
    earlier_same = (owner_index[:, None] == owner_index[None, :]) & (
        position[None, :] < position[:, None]
    )
    slot_index = jnp.sum(earlier_same.astype(jnp.int32), axis=1)
    requests = (
        jnp.full((owner_count, slot_cap), -1, jnp.int32).at[owner_index, slot_index].set(pool_row)
    )
    wanted = lax.all_to_all(requests, ("grp", "blk"), split_axis=0, concat_axis=0, tiled=True)
    served = serve_rows(hard_pool, wanted)
    fetched = lax.all_to_all(served, ("grp", "blk"), split_axis=0, concat_axis=0, tiled=True)
    hard_rows = fetched[owner_index, slot_index]
    hard_score = jnp.einsum("rd,rd->r", own_source, hard_rows, preferred_element_type=jnp.float32)
    top_start = jnp.full((row_count,), neg_fill, jnp.float32)
    top_start = lax.dynamic_update_slice_in_dim(top_start, hard_score, own_start, 0)
    total_start = jnp.zeros((row_count,), jnp.float32)
    total_start = lax.dynamic_update_slice_in_dim(
        total_start, jnp.ones((tgt_rows,), jnp.float32), own_start, 0
    )
    positive_start = jnp.zeros((row_count,), jnp.float32)

    def absorb(partials, tgt_block, step_index):
        row_top, row_total, positive_sum = partials
        adjusted, positive = adjusted_scores(tgt_block, step_index)
        new_top = jnp.maximum(row_top, jnp.max(adjusted, axis=1))
        row_total = row_total * jnp.exp(row_top - new_top) + jnp.sum(
            jnp.exp(adjusted - new_top[:, None]), axis=1
        )
        positive_sum = positive_sum + jnp.sum(jnp.where(positive, adjusted, 0.0), axis=1)
        return (new_top, row_total, positive_sum)

    def forward(step_index, loop_state):
        tgt_block, partials, stored = loop_state
        partials = absorb(partials, tgt_block, step_index)
        stored = lax.dynamic_update_index_in_dim(stored, tgt_block, step_index, 0)
        tgt_block = shifted(tgt_block, "blk", 1)
        return (tgt_block, partials, stored)

    stored = jnp.zeros((blk_count, tgt_rows, width), target_emb.dtype)
    start_state = (target_emb, (top_start, total_start, positive_start), stored)
    tgt_block, partials, stored = lax.fori_loop(0, blk_count - 1, forward, start_state)
    last_step = blk_count - 1
    partials = absorb(partials, tgt_block, last_step)
    stored = lax.dynamic_update_index_in_dim(stored, tgt_block, last_step, 0)
    row_top, row_total, positive_sum = merged(partials, "grp", combine)
    log_total = row_top + jnp.log(row_total)
    row_loss = log_total - positive_sum

    def backward(step_index, loop_state):
        grad_block, source_acc = loop_state
        tgt_block = lax.dynamic_index_in_dim(stored, step_index, 0, keepdims=False)
        adjusted, positive = adjusted_scores(tgt_block, step_index)
        prob_tile = (jnp.exp(adjusted - log_total[:, None]) - positive.astype(jnp.float32)).astype(
            jnp.bfloat16
        )
        source_acc = source_acc + jnp.einsum(
            "rt,td->rd", prob_tile, tgt_block, preferred_element_type=jnp.float32
        )
        grad_block = grad_block + jnp.einsum(
            "rt,rd->td", prob_tile, source_emb, preferred_element_type=jnp.float32
        )
        grad_block = shifted(grad_block, "blk", 1)
        return (grad_block, source_acc)

    back_start = (
        jnp.zeros((tgt_rows, width), jnp.float32),
        jnp.zeros((row_count, width), jnp.float32),
    )
    target_grad, source_acc = lax.fori_loop(0, blk_count, backward, back_start)
    own_total = lax.dynamic_slice_in_dim(log_total, own_start, tgt_rows, 0)
    hard_prob = jnp.exp(hard_score - own_total)
    own_acc = lax.dynamic_slice_in_dim(source_acc, own_start, tgt_rows, 0)
    own_acc = own_acc + hard_prob[:, None] * hard_rows.astype(jnp.float32)
    source_acc = lax.dynamic_update_slice_in_dim(source_acc, own_acc, own_start, 0)
    source_grad = lax.psum(source_acc, "grp")
    contribution = hard_prob[:, None] * own_source.astype(jnp.float32)
    outgoing = (
        jnp.zeros((owner_count, slot_cap, width), jnp.float32)
        .at[owner_index, slot_index]
        .set(contribution)
    )
    incoming = lax.all_to_all(outgoing, ("grp", "blk"), split_axis=0, concat_axis=0, tiled=True)
    is_valid = wanted >= 0
    kept = jnp.where(is_valid[..., None], incoming, 0.0).reshape(owner_count * slot_cap, width)
    pool_grad = (
        jnp.zeros((tgt_rows, width), jnp.float32).at[jnp.maximum(wanted, 0).reshape(-1)].add(kept)
    )
    return (row_loss, source_grad, target_grad, pool_grad)


def solution(mesh):
    in_specs = (
        P("blk", None),
        P(("grp", "blk"), None),
        P(("grp", "blk"), None),
        P("blk"),
        P("blk"),
        P(),
    )
    out_specs = (P("blk"), P("blk", None), P(("grp", "blk"), None), P(("grp", "blk"), None))
    return jax.shard_map(shards, mesh=mesh, in_specs=in_specs, out_specs=out_specs, check_vma=False)
```

profile of v0, /device:TPU:0, one launch (start us, length us, event | category | flops | bytes accessed | tf_op | source)
XLA Modules:
  0.0 403.5 jit_solution(15260221158382620578)
XLA Ops:
  8.2 10.5 %scatter_fusion = s32[32,12]{0,1:T(8,128)S(1)} fusion(s32[32,12]{0,1:T(8,128)S(1)} %broadcast_in_dim.189, s32[192]{0:T(256)S(1)} %bitcast.74, s32[192]{0:T(256)S(1)} %get-tuple-element.769), kind=kCustom, calls=%fused_computation.2 | custom fusion | bytes 3840 | tf_op jit(solution)/shard_map/scatter | solution.py:72
  18.8 14.2 %all_to_all.19 = s32[32,1,12]{2,1,0:T(1,128)S(1)} all-to-all(s32[32,1,12]{2,1,0:T(1,128)S(1)} %copy.33), channel_id=1, replica_groups=mesh['grp'=4,'blk'=8] {'grp','blk'}, dimensions={0} | all-to-all | bytes 3072 | tf_op jit(solution)/shard_map/all_to_all | solution.py:74
  37.7 3.3 all-to-all-start.1
  43.1 19.9 %all-to-all-done.1 = bf16[32,12,768]{2,1,0:T(8,128)(2,1)} async-done(((bf16[32,12,768]{2,1,0:T(8,128)(2,1)}), bf16[32,12,768]{2,1,0:T(8,128)(2,1)}, u32[]{:S(2)}, u32[]{:S(2)}) %all-to-all-start.1) | async-done | bytes 589856 | tf_op jit(solution)/shard_map/all_to_all | solution.py:76
  64.3 3.0 gather_fusion.1
  70.4 56.2 %while.57 = (s32[]{:T(128)}, bf16[192,768]{1,0:T(8,128)(2,1)S(1)}, f32[768]{0:T(1024)S(1)}, f32[768]{0:T(1024)S(1)}, f32[768]{0:T(1024)}, /*index=5*/bf16[8,192,...) while((s32[]{:T(128)}, bf16[192,768]{1,0:T(8,128)(2,1)S(1)}, ...), condition=%wide.region_7.8_spmd.clone, body=%wide.region_3.7_spmd.clone.sunk | while | flops 227822800 | bytes 5105316 | solution.py:106
  73.4 5.1 %collective-permute-done = bf16[192,768]{1,0:T(8,128)(2,1)S(1)} collective-permute-done((bf16[192,768]{1,0:T(8,128)(2,1)S(1)}, bf16[192,768]{1,0:T(8,128)(2,1)S(1)}, u32[]{:S(2)}, u32[]{:S(2)}) %collective-permute-start) | collective-permute-done | bytes 294944 | tf_op jit(solution)/shard_map/while/body/eval_jaxpr/ppermute | solution.py:12
  81.4 5.1 %collective-permute-done = bf16[192,768]{1,0:T(8,128)(2,1)S(1)} collective-permute-done((bf16[192,768]{1,0:T(8,128)(2,1)S(1)}, bf16[192,768]{1,0:T(8,128)(2,1)S(1)}, u32[]{:S(2)}, u32[]{:S(2)}) %collective-permute-start) | collective-permute-done | bytes 294944 | tf_op jit(solution)/shard_map/while/body/eval_jaxpr/ppermute | solution.py:12
  89.5 5.1 %collective-permute-done = bf16[192,768]{1,0:T(8,128)(2,1)S(1)} collective-permute-done((bf16[192,768]{1,0:T(8,128)(2,1)S(1)}, bf16[192,768]{1,0:T(8,128)(2,1)S(1)}, u32[]{:S(2)}, u32[]{:S(2)}) %collective-permute-start) | collective-permute-done | bytes 294944 | tf_op jit(solution)/shard_map/while/body/eval_jaxpr/ppermute | solution.py:12
  97.5 5.1 %collective-permute-done = bf16[192,768]{1,0:T(8,128)(2,1)S(1)} collective-permute-done((bf16[192,768]{1,0:T(8,128)(2,1)S(1)}, bf16[192,768]{1,0:T(8,128)(2,1)S(1)}, u32[]{:S(2)}, u32[]{:S(2)}) %collective-permute-start) | collective-permute-done | bytes 294944 | tf_op jit(solution)/shard_map/while/body/eval_jaxpr/ppermute | solution.py:12
  105.5 5.1 %collective-permute-done = bf16[192,768]{1,0:T(8,128)(2,1)S(1)} collective-permute-done((bf16[192,768]{1,0:T(8,128)(2,1)S(1)}, bf16[192,768]{1,0:T(8,128)(2,1)S(1)}, u32[]{:S(2)}, u32[]{:S(2)}) %collective-permute-start) | collective-permute-done | bytes 294944 | tf_op jit(solution)/shard_map/while/body/eval_jaxpr/ppermute | solution.py:12
  113.5 5.1 %collective-permute-done = bf16[192,768]{1,0:T(8,128)(2,1)S(1)} collective-permute-done((bf16[192,768]{1,0:T(8,128)(2,1)S(1)}, bf16[192,768]{1,0:T(8,128)(2,1)S(1)}, u32[]{:S(2)}, u32[]{:S(2)}) %collective-permute-start) | collective-permute-done | bytes 294944 | tf_op jit(solution)/shard_map/while/body/eval_jaxpr/ppermute | solution.py:12
  121.6 5.1 %collective-permute-done = bf16[192,768]{1,0:T(8,128)(2,1)S(1)} collective-permute-done((bf16[192,768]{1,0:T(8,128)(2,1)S(1)}, bf16[192,768]{1,0:T(8,128)(2,1)S(1)}, u32[]{:S(2)}, u32[]{:S(2)}) %collective-permute-start) | collective-permute-done | bytes 294944 | tf_op jit(solution)/shard_map/while/body/eval_jaxpr/ppermute | solution.py:12
  128.5 7.2 %all-gather.3 = f32[4,1,768]{2,1,0:T(1,128)S(1)} all-gather(f32[1,1,768]{2,1,0:T(1,128)S(1)} %reshape.152), channel_id=2, replica_groups=mesh['grp'=4,'blk'=8] {'grp'}, dimensions={0}, use_global_device_ids=true | all-gather | bytes 15360 | tf_op jit(solution)/shard_map/all_gather | solution.py:16
  135.9 8.1 %all-gather.4 = f32[4,1,768]{2,1,0:T(1,128)S(1)} all-gather(f32[1,1,768]{2,1,0:T(1,128)S(1)} %reshape.154), channel_id=3, replica_groups=mesh['grp'=4,'blk'=8] {'grp'}, dimensions={0}, use_global_device_ids=true | all-gather | bytes 15360 | tf_op jit(solution)/shard_map/all_gather | solution.py:16
  144.1 7.3 %all-gather.5 = f32[4,1,768]{2,1,0:T(1,128)S(1)} all-gather(f32[1,1,768]{2,1,0:T(1,128)S(1)} %reshape.156), channel_id=4, replica_groups=mesh['grp'=4,'blk'=8] {'grp'}, dimensions={0}, use_global_device_ids=true | all-gather | bytes 15360 | tf_op jit(solution)/shard_map/all_gather | solution.py:16
  153.3 116.5 %while.58 = (s32[]{:T(128)}, f32[192,768]{1,0:T(8,128)S(1)}, f32[768,768]{1,0:T(8,128)S(1)}, bf16[8,192,768]{2,1,0:T(8,128)(2,1)}, bf16[768,768]{1,0:T(8,128)(2,...) while((s32[]{:T(128)}, f32[192,768]{1,0:T(8,128)S(1)}, ...), condition=%wide.region_14.15_spmd.clone, body=%wide.region_13.14_spmd.clone.sunk | while | flops 681837504 | bytes 16825220 | solution.py:134
  158.5 9.5 %collective-permute-done.1 = f32[192,768]{1,0:T(8,128)S(1)} collective-permute-done((f32[192,768]{1,0:T(8,128)}, f32[192,768]{1,0:T(8,128)S(1)}, u32[]{:S(2)}, u32[]{:S(2)}) %collective-permute-start.1) | collective-permute-done | bytes 589856 | tf_op jit(solution)/shard_map/while/body/eval_jaxpr/ppermute | solution.py:12
  173.1 9.5 %collective-permute-done.1 = f32[192,768]{1,0:T(8,128)S(1)} collective-permute-done((f32[192,768]{1,0:T(8,128)}, f32[192,768]{1,0:T(8,128)S(1)}, u32[]{:S(2)}, u32[]{:S(2)}) %collective-permute-start.1) | collective-permute-done | bytes 589856 | tf_op jit(solution)/shard_map/while/body/eval_jaxpr/ppermute | solution.py:12
  187.6 9.5 %collective-permute-done.1 = f32[192,768]{1,0:T(8,128)S(1)} collective-permute-done((f32[192,768]{1,0:T(8,128)}, f32[192,768]{1,0:T(8,128)S(1)}, u32[]{:S(2)}, u32[]{:S(2)}) %collective-permute-start.1) | collective-permute-done | bytes 589856 | tf_op jit(solution)/shard_map/while/body/eval_jaxpr/ppermute | solution.py:12
  202.2 9.5 %collective-permute-done.1 = f32[192,768]{1,0:T(8,128)S(1)} collective-permute-done((f32[192,768]{1,0:T(8,128)}, f32[192,768]{1,0:T(8,128)S(1)}, u32[]{:S(2)}, u32[]{:S(2)}) %collective-permute-start.1) | collective-permute-done | bytes 589856 | tf_op jit(solution)/shard_map/while/body/eval_jaxpr/ppermute | solution.py:12
  216.7 9.5 %collective-permute-done.1 = f32[192,768]{1,0:T(8,128)S(1)} collective-permute-done((f32[192,768]{1,0:T(8,128)}, f32[192,768]{1,0:T(8,128)S(1)}, u32[]{:S(2)}, u32[]{:S(2)}) %collective-permute-start.1) | collective-permute-done | bytes 589856 | tf_op jit(solution)/shard_map/while/body/eval_jaxpr/ppermute | solution.py:12
  231.3 9.5 %collective-permute-done.1 = f32[192,768]{1,0:T(8,128)S(1)} collective-permute-done((f32[192,768]{1,0:T(8,128)}, f32[192,768]{1,0:T(8,128)S(1)}, u32[]{:S(2)}, u32[]{:S(2)}) %collective-permute-start.1) | collective-permute-done | bytes 589856 | tf_op jit(solution)/shard_map/while/body/eval_jaxpr/ppermute | solution.py:12
  245.8 9.5 %collective-permute-done.1 = f32[192,768]{1,0:T(8,128)S(1)} collective-permute-done((f32[192,768]{1,0:T(8,128)}, f32[192,768]{1,0:T(8,128)S(1)}, u32[]{:S(2)}, u32[]{:S(2)}) %collective-permute-start.1) | collective-permute-done | bytes 589856 | tf_op jit(solution)/shard_map/while/body/eval_jaxpr/ppermute | solution.py:12
  260.4 9.5 %collective-permute-done.1 = f32[192,768]{1,0:T(8,128)S(1)} collective-permute-done((f32[192,768]{1,0:T(8,128)}, f32[192,768]{1,0:T(8,128)S(1)}, u32[]{:S(2)}, u32[]{:S(2)}) %collective-permute-start.1) | collective-permute-done | bytes 589856 | tf_op jit(solution)/shard_map/while/body/eval_jaxpr/ppermute | solution.py:12
  273.2 26.9 %scatter_fusion.1 = f32[32,12,768]{2,0,1:T(8,128)} fusion(f32[32,12,768]{2,0,1:T(8,128)} %broadcast_in_dim.203, s32[192]{0:T(256)S(1)} %bitcast.75, f32[192,768]{1,0:T(8,128)} %get-tuple-element.770), kind=kCustom, calls=%fused_computation.3 | custom fusion | bytes 1771008 | tf_op jit(solution)/shard_map/scatter | solution.py:145
  300.1 3.1 copy.40
  303.2 2.7 all-to-all-start.2
  306.7 38.1 %all-to-all-done.2 = f32[32,12,768]{2,1,0:T(8,128)S(1)} async-done(((f32[32,12,768]{2,1,0:T(8,128)}), f32[32,12,768]{2,1,0:T(8,128)S(1)}, u32[]{:S(2)}, u32[]{:S(2)}) %all-to-all-start.2) | async-done | bytes 1179680 | tf_op jit(solution)/shard_map/all_to_all | solution.py:147
  347.5 4.6 %scatter_custom_fusion.2 = f32[192,768]{1,0:T(8,128)} fusion(s32[384]{0:T(512)} %copy-done.13, f32[384,768]{1,0:T(8,128)} %reshape.133, f32[]{:T(128)} %constant.231.clone.1), kind=kCustom, calls=%fused_computation.59 | custom fusion | flops 294912 | bytes 590336 | tf_op jit(solution)/shard_map/scatter-add | solution.py:151
  352.0 40.6 %all-reduce.2.cloned.1.call-done = f32[768,768]{1,0:T(8,128)} async-done(((f32[768,768]{1,0:T(8,128)}), f32[768,768]{1,0:T(8,128)}) %all-reduce.2.cloned.1.call-update) | async-done | bytes 2359312 | tf_op jit(solution)/shard_map/psum | solution.py:140
  392.6 3.2 copy.111
  (259 shorter events, 84.2 us)
Async XLA Ops:
  7.2 26.7 %copy-start = (bf16[192,768]{1,0:T(8,128)(2,1)S(1)}, bf16[192,768]{1,0:T(8,128)(2,1)}, u32[]{:S(2)}) copy-start(bf16[192,768]{1,0:T(8,128)(2,1)} %param.14) | copy-start | bytes 884740
  36.5 5.9 %copy-start.14 = (s32[768]{0:T(1024)S(1)}, s32[768]{0:T(1024)}, u32[]{:S(2)}) copy-start(s32[768]{0:T(1024)} %param.16) | copy-start | bytes 9220
  36.5 5.9 %copy-start.16 = (f32[109]{0:T(128)S(1)}, f32[109]{0:T(128)}, u32[]{:S(2)}) copy-start(f32[109]{0:T(128)} %param.17) | copy-start | bytes 1312
  37.7 25.3 %all-to-all-start.1 = ((bf16[32,12,768]{2,1,0:T(8,128)(2,1)}), bf16[32,12,768]{2,1,0:T(8,128)(2,1)}, u32[]{:S(2)}, u32[]{:S(2)}) async-start(bf16[32,12,768]{2,1,0:T(8,128)(2,1)} %copy.38), calls=%async_computation.1 | async-start | bytes 1572864 | tf_op jit(solution)/shard_map/all_to_all | solution.py:76
  70.5 8.0 %collective-permute-start = (bf16[192,768]{1,0:T(8,128)(2,1)S(1)}, bf16[192,768]{1,0:T(8,128)(2,1)S(1)}, u32[]{:S(2)}, u32[]{:S(2)}) collective-permute-start(bf16[192,768]{1,0:T(8,128)(2,1)S(1)} %copy.72), channel_id=1, source_target_pairs={{7,0},{0,1},{1,2},{2,3},{3,4},{4,5},{5,6},{6,7},{15,8},{8,9},{9,10... | collective-permute-start | bytes 884744 | tf_op jit(solution)/shard_map/while/body/eval_jaxpr/ppermute | solution.py:12
  78.5 8.0 %collective-permute-start = (bf16[192,768]{1,0:T(8,128)(2,1)S(1)}, bf16[192,768]{1,0:T(8,128)(2,1)S(1)}, u32[]{:S(2)}, u32[]{:S(2)}) collective-permute-start(bf16[192,768]{1,0:T(8,128)(2,1)S(1)} %copy.72), channel_id=1, source_target_pairs={{7,0},{0,1},{1,2},{2,3},{3,4},{4,5},{5,6},{6,7},{15,8},{8,9},{9,10... | collective-permute-start | bytes 884744 | tf_op jit(solution)/shard_map/while/body/eval_jaxpr/ppermute | solution.py:12
  86.5 8.0 %collective-permute-start = (bf16[192,768]{1,0:T(8,128)(2,1)S(1)}, bf16[192,768]{1,0:T(8,128)(2,1)S(1)}, u32[]{:S(2)}, u32[]{:S(2)}) collective-permute-start(bf16[192,768]{1,0:T(8,128)(2,1)S(1)} %copy.72), channel_id=1, source_target_pairs={{7,0},{0,1},{1,2},{2,3},{3,4},{4,5},{5,6},{6,7},{15,8},{8,9},{9,10... | collective-permute-start | bytes 884744 | tf_op jit(solution)/shard_map/while/body/eval_jaxpr/ppermute | solution.py:12
  88.7 5.8 %copy-start.6 = (f32[768]{0:T(1024)}, f32[768]{0:T(1024)S(1)}, u32[]{:S(2)}) copy-start(f32[768]{0:T(1024)S(1)} %get-tuple-element.1001) | copy-start | bytes 9220 | tf_op jit(solution)/shard_map/while
  94.6 8.0 %collective-permute-start = (bf16[192,768]{1,0:T(8,128)(2,1)S(1)}, bf16[192,768]{1,0:T(8,128)(2,1)S(1)}, u32[]{:S(2)}, u32[]{:S(2)}) collective-permute-start(bf16[192,768]{1,0:T(8,128)(2,1)S(1)} %copy.72), channel_id=1, source_target_pairs={{7,0},{0,1},{1,2},{2,3},{3,4},{4,5},{5,6},{6,7},{15,8},{8,9},{9,10... | collective-permute-start | bytes 884744 | tf_op jit(solution)/shard_map/while/body/eval_jaxpr/ppermute | solution.py:12
  96.7 5.8 %copy-start.6 = (f32[768]{0:T(1024)}, f32[768]{0:T(1024)S(1)}, u32[]{:S(2)}) copy-start(f32[768]{0:T(1024)S(1)} %get-tuple-element.1001) | copy-start | bytes 9220 | tf_op jit(solution)/shard_map/while
  102.6 8.0 %collective-permute-start = (bf16[192,768]{1,0:T(8,128)(2,1)S(1)}, bf16[192,768]{1,0:T(8,128)(2,1)S(1)}, u32[]{:S(2)}, u32[]{:S(2)}) collective-permute-start(bf16[192,768]{1,0:T(8,128)(2,1)S(1)} %copy.72), channel_id=1, source_target_pairs={{7,0},{0,1},{1,2},{2,3},{3,4},{4,5},{5,6},{6,7},{15,8},{8,9},{9,10... | collective-permute-start | bytes 884744 | tf_op jit(solution)/shard_map/while/body/eval_jaxpr/ppermute | solution.py:12
  104.8 5.8 %copy-start.6 = (f32[768]{0:T(1024)}, f32[768]{0:T(1024)S(1)}, u32[]{:S(2)}) copy-start(f32[768]{0:T(1024)S(1)} %get-tuple-element.1001) | copy-start | bytes 9220 | tf_op jit(solution)/shard_map/while
  110.6 8.0 %collective-permute-start = (bf16[192,768]{1,0:T(8,128)(2,1)S(1)}, bf16[192,768]{1,0:T(8,128)(2,1)S(1)}, u32[]{:S(2)}, u32[]{:S(2)}) collective-permute-start(bf16[192,768]{1,0:T(8,128)(2,1)S(1)} %copy.72), channel_id=1, source_target_pairs={{7,0},{0,1},{1,2},{2,3},{3,4},{4,5},{5,6},{6,7},{15,8},{8,9},{9,10... | collective-permute-start | bytes 884744 | tf_op jit(solution)/shard_map/while/body/eval_jaxpr/ppermute | solution.py:12
  112.8 5.8 %copy-start.6 = (f32[768]{0:T(1024)}, f32[768]{0:T(1024)S(1)}, u32[]{:S(2)}) copy-start(f32[768]{0:T(1024)S(1)} %get-tuple-element.1001) | copy-start | bytes 9220 | tf_op jit(solution)/shard_map/while
  118.6 8.0 %collective-permute-start = (bf16[192,768]{1,0:T(8,128)(2,1)S(1)}, bf16[192,768]{1,0:T(8,128)(2,1)S(1)}, u32[]{:S(2)}, u32[]{:S(2)}) collective-permute-start(bf16[192,768]{1,0:T(8,128)(2,1)S(1)} %copy.72), channel_id=1, source_target_pairs={{7,0},{0,1},{1,2},{2,3},{3,4},{4,5},{5,6},{6,7},{15,8},{8,9},{9,10... | collective-permute-start | bytes 884744 | tf_op jit(solution)/shard_map/while/body/eval_jaxpr/ppermute | solution.py:12
  120.8 5.8 %copy-start.6 = (f32[768]{0:T(1024)}, f32[768]{0:T(1024)S(1)}, u32[]{:S(2)}) copy-start(f32[768]{0:T(1024)S(1)} %get-tuple-element.1001) | copy-start | bytes 9220 | tf_op jit(solution)/shard_map/while
  126.6 9.1 %copy-start.10 = (s32[768]{0:T(1024)S(1)}, s32[768]{0:T(1024)}, u32[]{:S(2)}) copy-start(s32[768]{0:T(1024)} %iota_add_fusion.4) | copy-start | bytes 9220
  126.6 9.1 %copy-start.15 = (s32[192]{0:T(256)S(1)}, s32[192]{0:T(256)}, u32[]{:S(2)}) copy-start(s32[192]{0:T(256)} %iota_add_fusion.5) | copy-start | bytes 2308
  126.6 17.5 %copy-start.7 = (f32[768]{0:T(1024)S(1)}, f32[768]{0:T(1024)}, u32[]{:S(2)}) copy-start(f32[768]{0:T(1024)} %get-tuple-element.607) | copy-start | bytes 9220
  126.6 25.8 %copy-start.12 = (f32[192]{0:T(256)S(1)}, f32[192]{0:T(256)}, u32[]{:S(2)}) copy-start(f32[192]{0:T(256)} %copy-done.11) | copy-start | bytes 2308
  156.6 11.3 %collective-permute-start.1 = (f32[192,768]{1,0:T(8,128)}, f32[192,768]{1,0:T(8,128)S(1)}, u32[]{:S(2)}, u32[]{:S(2)}) collective-permute-start(f32[192,768]{1,0:T(8,128)} %convolution_add_fusion.2), channel_id=1, source_target_pairs={{7,0},{0,1},{1,2},{2,3},{3,4},{4,5},{5,6},{6,7},{15,8},{8,9},{9,10... | collective-permute-start | bytes 1769480 | tf_op jit(solution)/shard_map/while/body/eval_jaxpr/ppermute | solution.py:12
  171.2 11.3 %collective-permute-start.1 = (f32[192,768]{1,0:T(8,128)}, f32[192,768]{1,0:T(8,128)S(1)}, u32[]{:S(2)}, u32[]{:S(2)}) collective-permute-start(f32[192,768]{1,0:T(8,128)} %convolution_add_fusion.2), channel_id=1, source_target_pairs={{7,0},{0,1},{1,2},{2,3},{3,4},{4,5},{5,6},{6,7},{15,8},{8,9},{9,10... | collective-permute-start | bytes 1769480 | tf_op jit(solution)/shard_map/while/body/eval_jaxpr/ppermute | solution.py:12
  185.8 11.3 %collective-permute-start.1 = (f32[192,768]{1,0:T(8,128)}, f32[192,768]{1,0:T(8,128)S(1)}, u32[]{:S(2)}, u32[]{:S(2)}) collective-permute-start(f32[192,768]{1,0:T(8,128)} %convolution_add_fusion.2), channel_id=1, source_target_pairs={{7,0},{0,1},{1,2},{2,3},{3,4},{4,5},{5,6},{6,7},{15,8},{8,9},{9,10... | collective-permute-start | bytes 1769480 | tf_op jit(solution)/shard_map/while/body/eval_jaxpr/ppermute | solution.py:12
  200.3 11.3 %collective-permute-start.1 = (f32[192,768]{1,0:T(8,128)}, f32[192,768]{1,0:T(8,128)S(1)}, u32[]{:S(2)}, u32[]{:S(2)}) collective-permute-start(f32[192,768]{1,0:T(8,128)} %convolution_add_fusion.2), channel_id=1, source_target_pairs={{7,0},{0,1},{1,2},{2,3},{3,4},{4,5},{5,6},{6,7},{15,8},{8,9},{9,10... | collective-permute-start | bytes 1769480 | tf_op jit(solution)/shard_map/while/body/eval_jaxpr/ppermute | solution.py:12
  214.9 11.3 %collective-permute-start.1 = (f32[192,768]{1,0:T(8,128)}, f32[192,768]{1,0:T(8,128)S(1)}, u32[]{:S(2)}, u32[]{:S(2)}) collective-permute-start(f32[192,768]{1,0:T(8,128)} %convolution_add_fusion.2), channel_id=1, source_target_pairs={{7,0},{0,1},{1,2},{2,3},{3,4},{4,5},{5,6},{6,7},{15,8},{8,9},{9,10... | collective-permute-start | bytes 1769480 | tf_op jit(solution)/shard_map/while/body/eval_jaxpr/ppermute | solution.py:12
  229.4 11.3 %collective-permute-start.1 = (f32[192,768]{1,0:T(8,128)}, f32[192,768]{1,0:T(8,128)S(1)}, u32[]{:S(2)}, u32[]{:S(2)}) collective-permute-start(f32[192,768]{1,0:T(8,128)} %convolution_add_fusion.2), channel_id=1, source_target_pairs={{7,0},{0,1},{1,2},{2,3},{3,4},{4,5},{5,6},{6,7},{15,8},{8,9},{9,10... | collective-permute-start | bytes 1769480 | tf_op jit(solution)/shard_map/while/body/eval_jaxpr/ppermute | solution.py:12
  244.0 11.3 %collective-permute-start.1 = (f32[192,768]{1,0:T(8,128)}, f32[192,768]{1,0:T(8,128)S(1)}, u32[]{:S(2)}, u32[]{:S(2)}) collective-permute-start(f32[192,768]{1,0:T(8,128)} %convolution_add_fusion.2), channel_id=1, source_target_pairs={{7,0},{0,1},{1,2},{2,3},{3,4},{4,5},{5,6},{6,7},{15,8},{8,9},{9,10... | collective-permute-start | bytes 1769480 | tf_op jit(solution)/shard_map/while/body/eval_jaxpr/ppermute | solution.py:12
  258.6 11.3 %collective-permute-start.1 = (f32[192,768]{1,0:T(8,128)}, f32[192,768]{1,0:T(8,128)S(1)}, u32[]{:S(2)}, u32[]{:S(2)}) collective-permute-start(f32[192,768]{1,0:T(8,128)} %convolution_add_fusion.2), channel_id=1, source_target_pairs={{7,0},{0,1},{1,2},{2,3},{3,4},{4,5},{5,6},{6,7},{15,8},{8,9},{9,10... | collective-permute-start | bytes 1769480 | tf_op jit(solution)/shard_map/while/body/eval_jaxpr/ppermute | solution.py:12
  271.9 28.2 %copy-start.1 = (f32[768,768]{1,0:T(8,128)}, f32[768,768]{1,0:T(8,128)S(1)}, u32[]{:S(2)}) copy-start(f32[768,768]{1,0:T(8,128)S(1)} %get-tuple-element.771) | copy-start | bytes 7077892
  303.2 41.6 %all-to-all-start.2 = ((f32[32,12,768]{2,1,0:T(8,128)}), f32[32,12,768]{2,1,0:T(8,128)S(1)}, u32[]{:S(2)}, u32[]{:S(2)}) async-start(f32[32,12,768]{2,1,0:T(8,128)} %copy.40), calls=%async_computation.2 | async-start | bytes 3145728 | tf_op jit(solution)/shard_map/all_to_all | solution.py:147
  305.9 38.9 %copy-start.9 = (pred[32,12]{0,1:T(8,128)(4,1)S(1)}, pred[32,12]{0,1:T(8,128)(4,1)}, u32[]{:S(2)}) copy-start(pred[32,12]{0,1:T(8,128)(4,1)} %copy-done.8) | copy-start | bytes 1156
  305.9 86.7 %all-reduce.2.cloned.1.call-start = ((), (), s32[]{:S(2)}) async-start(), calls=%async_computation.3 | async-start | bytes 4718592 | tf_op jit(solution)/shard_map/psum | solution.py:140
  (22 other events, 54.0 us)
Sparse Core Ops, SparseCore 0:
  310.5 82.0 all-reduce.1
where the time goes:
time: 406 us; the launch traced here: 403 us
  waiting for transfers between devices  210 us (52%)
  local copies, waits for them, and re-layouts  64.8 us (16%)
  matrix products  55.2 us (14%)
  blocking collectives  36.9 us (9%)
  between operations  14.5 us (4%)
  other arithmetic  14 us (3%)
  starting transfers between devices  6.49 us (2%)
    ppermute x15, waiting for transfers between devices, shifted(): return lax.ppermute(block, axis, route)  111 us
    psum x1, waiting for transfers between devices, shards(): source_grad = lax.psum(source_acc, 'grp')  40.6 us
    all_to_all x1, waiting for transfers between devices, shards(): lax.all_to_all(outgoing, ('grp', 'blk'), split_axis=0, concat_axis=0, til...  38.1 us
    dot_general x16, matrix products, adjusted_scores(): jnp.einsum('rd,td->rt', source_emb, tgt_block, preferred_element_type=jnp...  30.7 us
    scatter x2, local copies, waits for them, and re-layouts, shards(): outgoing = jnp.zeros((owner_count, slot_cap, width), jnp.float32).at[owne...  30 us
    all_gather x3, blocking collectives, merged(): pieces = jax.tree.map(lambda part: lax.all_gather(part, axis), value)  22.6 us
    all_to_all x1, waiting for transfers between devices, shards(): lax.all_to_all(served, ('grp', 'blk'), split_axis=0, concat_axis=0, tiled...  19.9 us
    dot_general x8, matrix products, backward(): jnp.einsum('rt,td->rd', prob_tile, tgt_block, preferred_element_type=jnp....  14.7 us
  transfers between devices with their start and end apart: 18, of which 18 were waited for; matrix products, arithmetic and copies ran while one was open for 11% of the time, Pallas kernels for 0%

commit v1 on v0

v1 whole, which is shorter than its diff:
```python
import functools

import jax
import jax.numpy as jnp
from jax import lax
from jax.experimental import pallas as pl
from jax.experimental.pallas import tpu as pltpu
from jax.sharding import PartitionSpec as P

neg_fill = -1e30
f32 = jnp.float32
bf16 = jnp.bfloat16
MESH = pl.DeviceIdType.MESH


def dot_nt(a, b):
    return lax.dot_general(a, b, (((1,), (1,)), ((), ())), preferred_element_type=f32)


def dot_tn(a, b):
    return lax.dot_general(a, b, (((0,), (0,)), ((), ())), preferred_element_type=f32)


def dot_nn(a, b):
    return lax.dot_general(a, b, (((1,), (0,)), ((), ())), preferred_element_type=f32)


def kernel(
    dims,
    src, tgt, pool, rows_in, margin_col,
    loss_out, sgrad, tgrad, pgrad,
    tall, adj, prob, sel, want_send, want_recv, picks, slots_send, slots_recv, hp_send, hp_recv,
    stats, sg_send, sg_recv, sib_send, sib_recv, rs_send, rs_recv,
    t_ss, t_rs, fw_ss, w_ss, w_rs, p_ss, p_rs, s_ss, s_rs, h_ss, h_rs, st_ss, st_rs,
    q_ss, q_rs, a_ss, a_rs, b_ss, b_rs, r_ss, r_rs,
):
    B, G, M, T, D, cap = dims
    Z = B // 2
    N1 = B * T
    W = 256
    b = lax.axis_index("blk")
    g = lax.axis_index("grp")
    z = b // 2
    c = b % 2
    sib = z * 2 + (1 - c)

    def blk_of(dz, core):
        return ((z + dz) % Z) * 2 + core

    def trows(j):
        return pl.ds(pl.multiple_of(j * T, T), T)

    def frows(j):
        return pl.ds(pl.multiple_of(N1 + j * cap, 16), cap)

    def crows(j):
        return pl.ds(pl.multiple_of(j * cap, 16), cap)

    def to_blk(src_ref, dst_ref, ss, rs, peer):
        return pltpu.make_async_remote_copy(
            src_ref=src_ref, dst_ref=dst_ref, send_sem=ss, recv_sem=rs,
            device_id={"blk": peer}, device_id_type=MESH,
        )

    def to_grp(src_ref, dst_ref, ss, rs, peer):
        return pltpu.make_async_remote_copy(
            src_ref=src_ref, dst_ref=dst_ref, send_sem=ss, recv_sem=rs,
            device_id={"grp": peer}, device_id_type=MESH,
        )

    barrier = pltpu.get_barrier_semaphore()
    for k in range(1, B):
        pl.semaphore_signal(barrier, inc=1, device_id={"blk": (b + k) % B}, device_id_type=MESH)
    for k in range(1, G):
        pl.semaphore_signal(barrier, inc=1, device_id={"grp": (g + k) % G}, device_id_type=MESH)

    owner_row = rows_in[0:1, :]
    loc_row = rows_in[1:2, :]
    present = owner_row >= 0
    col_id = lax.broadcasted_iota(jnp.int32, (T, M), 1)
    row_id = lax.broadcasted_iota(jnp.int32, (T, M), 0)

    R = max(B, 16)
    named = owner_row == lax.broadcasted_iota(jnp.int32, (R, M), 0)
    named_hot = jnp.where(named, 1.0, 0.0).astype(bf16)
    before = jnp.zeros((R, M), f32)
    for n in range(M // W):
        earlier = lax.broadcasted_iota(jnp.int32, (W, M), 0) + n * W < lax.broadcasted_iota(
            jnp.int32, (W, M), 1
        )
        step = jnp.where(earlier, 1.0, 0.0).astype(bf16)
        before = before + dot_nn(named_hot[:, n * W : (n + 1) * W], step)
    rank = jnp.sum(jnp.where(named, before, 0.0), axis=0, keepdims=True).astype(jnp.int32)
    slot = jnp.where(present, owner_row * cap + rank, -1)

    slot_id = lax.broadcasted_iota(jnp.int32, (cap, M), 0)
    loc8 = jnp.broadcast_to((loc_row + 1).astype(f32).astype(bf16), (8, M))

    def fill_sel(j, carry):
        hot = jnp.where(slot == slot_id + j * cap, 1.0, 0.0).astype(bf16)
        sel[crows(j), :] = hot
        want_send[j, :, 0:cap] = dot_nt(loc8, hot) - 1.0
        return carry

    lax.fori_loop(0, B, fill_sel, 0)

    pl.semaphore_wait(barrier, B - 1 + G - 1)

    sends = []
    for k in range(1, B):
        peer = (b + k) % B
        cp = to_blk(want_send.at[peer], want_recv.at[b], w_ss.at[k], w_rs.at[b], peer)
        cp.start()
        sends.append(cp)
    cp = to_blk(tgt, tall.at[trows(b)], t_ss.at[0], t_rs.at[b], sib)
    cp.start()
    sends.append(cp)
    for dz in range(1, Z):
        cp = to_blk(tgt, tall.at[trows(b)], t_ss.at[dz], t_rs.at[b], blk_of(dz, c))
        cp.start()
        sends.append(cp)
    tall[trows(b), :] = tgt[...]
    want_recv[b] = want_send[b]

    lang_id = lax.broadcasted_iota(jnp.int32, (margin_col.shape[0], M), 0)
    margin_row = jnp.sum(
        jnp.where(rows_in[2:3, :] == lang_id, margin_col[...], 0.0), axis=0, keepdims=True
    )

    def hit(j):
        return row_id - col_id == b * M - (g * B + j) * T

    def score(j, carry):
        top, pos = carry
        s = dot_nt(tall[trows(j), :], src[...])
        diag = hit(j)
        s = s - jnp.where(diag, margin_row, 0.0)
        adj[trows(j), :] = s
        top = jnp.maximum(top, jnp.max(s, axis=0, keepdims=True))
        pos = pos + jnp.sum(jnp.where(diag, s, 0.0), axis=0, keepdims=True)
        return top, pos

    carry = (jnp.full((1, M), neg_fill, f32), jnp.zeros((1, M), f32))
    carry = score(b, carry)

    pool_id = lax.broadcasted_iota(jnp.int32, (T, cap), 0).astype(f32)
    for k in range(0, B):
        peer = (b + k) % B
        if k:
            to_blk(want_send.at[0], want_recv.at[peer], w_ss.at[0], w_rs.at[peer], peer).wait_recv()
        hot = jnp.where(pool_id == want_recv[peer, 0:1, 0:cap], 1.0, 0.0).astype(bf16)
        picked = dot_tn(hot, pool[...]).astype(bf16)
        if k == 0:
            tall[frows(b), :] = picked
        else:
            picks[k - 1] = picked
            cp = to_blk(picks.at[k - 1], tall.at[frows(b)], p_ss.at[k], p_rs.at[b], peer)
            cp.start()
            sends.append(cp)

    def wait_t(j):
        to_blk(tgt, tall.at[trows(j)], t_ss.at[0], t_rs.at[j], sib).wait_recv()

    wait_t(sib)
    carry = score(sib, carry)
    for dz in range(1, Z):
        near = blk_of(dz, c)
        wait_t(near)
        cp = to_blk(tall.at[trows(near)], tall.at[trows(near)], fw_ss.at[dz], t_rs.at[near], sib)
        cp.start()
        sends.append(cp)
        carry = score(near, carry)
    def fill_slots(j, carry):
        slots_send[j] = dot_nn(sel[crows(j), :], src[...]).astype(bf16)
        return carry

    lax.fori_loop(0, B, fill_slots, 0)
    for k in range(1, B):
        peer = (b + k) % B
        cp = to_blk(slots_send.at[peer], slots_recv.at[b], s_ss.at[k], s_rs.at[b], peer)
        cp.start()
        sends.append(cp)
    slots_recv[b] = slots_send[b]
    for dz in range(1, Z):
        far = blk_of(dz, 1 - c)
        wait_t(far)
        carry = score(far, carry)
    top, pos = carry
    for k in range(1, B):
        peer = (b + k) % B
        to_blk(picks.at[0], tall.at[frows(peer)], p_ss.at[0], p_rs.at[peer], peer).wait_recv()

    def hard_part(j, acc):
        s = dot_nt(tall[frows(j), :], src[...])
        return acc + jnp.sum(s * sel[crows(j), :].astype(f32), axis=0, keepdims=True)

    hard = lax.fori_loop(0, B, hard_part, jnp.zeros((1, M), f32))
    hard = jnp.where(present, hard, neg_fill)
    top = jnp.maximum(top, hard)

    def add_exp(j, acc):
        return acc + jnp.sum(jnp.exp(adj[trows(j), :] - top), axis=0, keepdims=True)

    total = jnp.where(present, jnp.exp(hard - top), 0.0)
    total = lax.fori_loop(0, B, add_exp, total)
    stats[g, 0:1, :] = top
    stats[g, 1:2, :] = total
    stats[g, 2:3, :] = pos
    for k in range(1, G):
        peer = (g + k) % G
        cp = to_grp(stats.at[g], stats.at[g], st_ss.at[k], st_rs.at[g], peer)
        cp.start()
        sends.append(cp)
    for k in range(1, G):
        peer = (g + k) % G
        to_grp(stats.at[g], stats.at[peer], st_ss.at[0], st_rs.at[peer], peer).wait_recv()
    all_top = stats[0, 0:1, :]
    for q in range(1, G):
        all_top = jnp.maximum(all_top, stats[q, 0:1, :])
    all_total = jnp.zeros((1, M), f32)
    all_pos = jnp.zeros((1, M), f32)
    for q in range(G):
        all_total = all_total + stats[q, 1:2, :] * jnp.exp(stats[q, 0:1, :] - all_top)
        all_pos = all_pos + stats[q, 2:3, :]
    log_total = all_top + jnp.log(all_total)
    loss_out[...] = log_total - all_pos
    hard_prob = jnp.where(present, jnp.exp(hard - log_total), 0.0)

    hp_hi = hard_prob.astype(bf16)
    rest = hard_prob - hp_hi.astype(f32)
    hp_mid = rest.astype(bf16)
    hp_lo = (rest - hp_mid.astype(f32)).astype(bf16)
    part_id = lax.broadcasted_iota(jnp.int32, (8, M), 0)
    hp8 = jnp.where(
        part_id == 0,
        hp_hi.astype(f32),
        jnp.where(
            part_id == 1, hp_mid.astype(f32), jnp.where(part_id == 2, hp_lo.astype(f32), 0.0)
        ),
    ).astype(bf16)

    def fill_hp(j, carry):
        hp_send[j, :, 0:cap] = dot_nt(hp8, sel[crows(j), :])
        return carry

    lax.fori_loop(0, B, fill_hp, 0)
    for k in range(1, B):
        peer = (b + k) % B
        cp = to_blk(hp_send.at[peer], hp_recv.at[b], h_ss.at[k], h_rs.at[b], peer)
        cp.start()
        sends.append(cp)
    hp_recv[b] = hp_send[b]

    def make_prob(j, carry):
        p = jnp.exp(adj[trows(j), :] - log_total) - jnp.where(hit(j), 1.0, 0.0)
        prob[trows(j), :] = p.astype(bf16)
        return carry

    lax.fori_loop(0, B, make_prob, 0)

    def fill_hard(j, carry):
        hot = sel[crows(j), :].astype(f32)
        prob[frows(j), :] = (hot * hp_hi.astype(f32)).astype(bf16)
        sel[crows(j), :] = (hot * hp_mid.astype(f32)).astype(bf16)
        return carry

    lax.fori_loop(0, B, fill_hard, 0)

    for dz in range(Z):
        j = blk_of(dz, 1 - c)
        sib_send[dz] = dot_nn(prob[trows(j), :], src[...]).astype(bf16)
        cp = to_blk(sib_send.at[dz], sib_recv.at[dz], b_ss.at[dz], b_rs.at[dz], sib)
        cp.start()
        sends.append(cp)
    for dz in list(range(1, Z)) + [0]:
        j = blk_of(dz, c)
        term = dot_nn(prob[trows(j), :], src[...])
        to_blk(sib_send.at[0], sib_recv.at[dz], b_ss.at[0], b_rs.at[dz], sib).wait_recv()
        term = term + sib_recv[dz].astype(f32)
        if dz == 0:
            tgrad[...] = term
        else:
            rs_send[dz - 1] = term.astype(bf16)
            cp = to_blk(rs_send.at[dz - 1], rs_recv.at[dz - 1], r_ss.at[dz], r_rs.at[dz], j)
            cp.start()
            sends.append(cp)

    V = W if N1 <= 2048 else W // 2
    for n in range(M // V):
        cols = pl.ds(n * V, V)
        part = dot_tn(prob[:, cols], tall[...])
        part = part + dot_tn(sel[:, cols], tall[pl.ds(N1, B * cap), :])
        sgrad[pl.ds(n * V, V), :] = part
    for k in range(1, G):
        peer = (g + k) % G
        sg_send[k - 1] = sgrad[trows(peer), :].astype(bf16)
        cp = to_grp(sg_send.at[k - 1], sg_recv.at[k - 1], q_ss.at[k], q_rs.at[k], peer)
        cp.start()
        sends.append(cp)

    acc = jnp.zeros((T, D), f32)
    for k in range(0, B):
        peer = (b + k) % B
        if k:
            to_blk(slots_send.at[0], slots_recv.at[peer], s_ss.at[0], s_rs.at[peer], peer).wait_recv()
            to_blk(hp_send.at[0], hp_recv.at[peer], h_ss.at[0], h_rs.at[peer], peer).wait_recv()
        hot = pool_id == want_recv[peer, 0:1, 0:cap]
        weight = jnp.sum(hp_recv[peer, :, 0:cap], axis=0, keepdims=True)
        hi = weight.astype(bf16).astype(f32)
        rows = slots_recv[peer]
        acc = acc + dot_nn(jnp.where(hot, hi, 0.0).astype(bf16), rows)
        acc = acc + dot_nn(jnp.where(hot, weight - hi, 0.0).astype(bf16), rows)
    pgrad[...] = acc

    own = sgrad[trows(g), :]
    for k in range(1, G):
        to_grp(sg_send.at[0], sg_recv.at[k - 1], q_ss.at[0], q_rs.at[k], (g + k) % G).wait_recv()
        own = own + sg_recv[k - 1].astype(f32)
    sgrad[trows(g), :] = own
    for k in range(1, G):
        peer = (g + k) % G
        cp = to_grp(sgrad.at[trows(g)], sgrad.at[trows(g)], a_ss.at[k], a_rs.at[g], peer)
        cp.start()
        sends.append(cp)

    final = tgrad[...]
    for dz in range(1, Z):
        to_blk(rs_send.at[0], rs_recv.at[dz - 1], r_ss.at[0], r_rs.at[dz], sib).wait_recv()
        final = final + rs_recv[dz - 1].astype(f32)
    tgrad[...] = final
    for k in range(1, G):
        peer = (g + k) % G
        to_grp(sgrad.at[trows(g)], sgrad.at[trows(peer)], a_ss.at[0], a_rs.at[peer], peer).wait_recv()
    for cp in sends:
        cp.wait_send()


def shards(source_emb, target_emb, hard_pool, hard_index, language, margin):
    M, D = source_emb.shape
    T = target_emb.shape[0]
    B = lax.axis_size("blk")
    G = lax.axis_size("grp")
    owners = B * G
    per_block = max(2, (2 * T + owners - 1) // owners)
    cap = -(-(per_block * (M // T)) // 16) * 16
    Z = B // 2
    g = lax.axis_index("grp")
    owner = hard_index // T
    local = jnp.where(owner // B == g, owner % B, -1)
    rows_in = jnp.stack([local, hard_index % T, language])
    dims = (B, G, M, T, D, cap)
    dma = pltpu.SemaphoreType.DMA
    vmem = pl.BlockSpec(memory_space=pltpu.VMEM)
    K = B * T + B * cap
    flops = 2 * M * D * (3 * B * T + 4 * B * cap)
    loss, sg, tg, pg = pl.pallas_call(
        functools.partial(kernel, dims),
        out_shape=[
            jax.ShapeDtypeStruct((1, M), f32),
            jax.ShapeDtypeStruct((M, D), f32),
            jax.ShapeDtypeStruct((T, D), f32),
            jax.ShapeDtypeStruct((T, D), f32),
        ],
        in_specs=[vmem] * 5,
        out_specs=[vmem] * 4,
        scratch_shapes=[
            pltpu.VMEM((K, D), bf16),
            pltpu.VMEM((B * T, M), f32),
            pltpu.VMEM((K, M), bf16),
            pltpu.VMEM((B * cap, M), bf16),
            pltpu.VMEM((B, 8, 128), f32),
            pltpu.VMEM((B, 8, 128), f32),
            pltpu.VMEM((B - 1, cap, D), bf16),
            pltpu.VMEM((B, cap, D), bf16),
            pltpu.VMEM((B, cap, D), bf16),
            pltpu.VMEM((B, 8, 128), f32),
            pltpu.VMEM((B, 8, 128), f32),
            pltpu.VMEM((G, 8, M), f32),
            pltpu.VMEM((G - 1, T, D), bf16),
            pltpu.VMEM((G - 1, T, D), bf16),
            pltpu.VMEM((Z, T, D), bf16),
            pltpu.VMEM((Z, T, D), bf16),
            pltpu.VMEM((Z - 1, T, D), bf16),
            pltpu.VMEM((Z - 1, T, D), bf16),
            dma((Z,)), dma((B,)), dma((Z,)),
            dma((B,)), dma((B,)), dma((B,)), dma((B,)),
            dma((B,)), dma((B,)), dma((B,)), dma((B,)),
            dma((G,)), dma((G,)),
            dma((G,)), dma((G,)), dma((G,)), dma((G,)),
            dma((Z,)), dma((Z,)), dma((Z,)), dma((Z,)),
        ],
        compiler_params=pltpu.CompilerParams(
            collective_id=0, has_side_effects=True, vmem_limit_bytes=63 * 1024 * 1024
        ),
        cost_estimate=pl.CostEstimate(
            flops=flops, bytes_accessed=8 * M * D, transcendentals=2 * B * T * M
        ),
        name="loss_kernel",
    )(
        source_emb, target_emb, hard_pool, rows_in,
        margin.reshape(margin.shape[0], 1),
    )
    return loss.reshape(M), sg, tg, pg


def solution(mesh):
    in_specs = (
        P("blk", None),
        P(("grp", "blk"), None),
        P(("grp", "blk"), None),
        P("blk"),
        P("blk"),
        P(),
    )
    out_specs = (P("blk"), P("blk", None), P(("grp", "blk"), None), P(("grp", "blk"), None))
    return jax.shard_map(shards, mesh=mesh, in_specs=in_specs, out_specs=out_specs, check_vma=False)
```

time: 406 us -> 125 us (0.31)
  the two profiles are of different devices: /device:TPU:0 before, /device:TPU:24 now
where the time goes in v1:
time: 125 us
  Pallas kernels  114 us (91%)
  local copies, waits for them, and re-layouts  7.04 us (6%)
  other arithmetic  2.6 us (2%)
    pallas_call x1, Pallas kernels, shards(): pl.pallas_call(functools.partial(kernel, dims), out_shape=[jax.ShapeDtype...  114 us
    unnamed x7, local copies, waits for them, and re-layouts  4.95 us

profile of v1, /device:TPU:24, one launch (start us, length us, event | category | flops | bytes accessed | tf_op | source)
XLA Modules:
  0.0 124.7 jit_solution(9420698882188081529)
XLA Ops:
  0.6 0.7 fusion.1
  1.4 0.7 stack.14
  2.1 0.6 pad_add_fusion.rows_in
  2.7 1.4 %copy.10.margin_col = f32[109,1]{1,0:T(8,128)} copy(f32[109,1]{0,1:T(1,128)} %bitcast.1) | data formatting | bytes 872 | tf_op jit(solution)/shard_map/reshape | solution.py:401
  4.1 114.4 %loss_kernel.1 = (f32[1,768]{1,0:T(1,128)}, f32[768,768]{1,0:T(8,128)}, f32[192,768]{1,0:T(8,128)}, f32[192,768]{1,0:T(8,128)}) custom-call(bf16[768,768]{1,0:T(8,128)(2,1)} %src.1, bf16[192,768]{1,0:T(8,128)(2,1)} %tgt.1, bf16[192,768]{1,0:T(8,128)(2,1)} %pool.1, s32[3,768]{1,0:T(4,128)} %pad_add_fusion.rows_in, f32[109,1]{1,0:T(8,128)} %copy.10.margin_col), custom_call_target="tpu_custom_call" | custom-call | flops 7247757312 | bytes 4718592 | tf_op jit(solution)/shard_map/loss_kernel/pallas_call | solution.py:356
  118.5 1.3 %reduce = f32[768]{0:T(1024)} reduce(f32[1,768]{1,0:T(1,128)} %get-tuple-element.8, f32[]{:T(128)} %constant.46), dimensions={0}, to_apply=%get-tuple-element.8.reduce_sub_computation | reduce | bytes 6148 | tf_op jit(solution)/shard_map/loss_kernel/pallas_call | solution.py:356
  119.7 0.0 copy-start.1
  119.7 0.0 copy-start
  119.7 3.3 %copy.14 = f32[768,768]{1,0:T(8,128)} copy(f32[768,768]{1,0:T(8,128)} %get-tuple-element.19) | data formatting | bytes 4718592
  123.1 0.0 copy-done.1
  123.1 0.8 copy.15
  123.9 0.0 copy-done
  123.9 0.8 copy.16
  (2 shorter events, 0.0 us)
Async XLA Ops:
  119.7 3.3 %copy-start.1 = (f32[192,768]{1,0:T(8,128)S(1)}, f32[192,768]{1,0:T(8,128)}, u32[]{:S(2)}) copy-start(f32[192,768]{1,0:T(8,128)} %get-tuple-element.20) | copy-start | bytes 1769476
  119.7 4.1 %copy-start = (f32[192,768]{1,0:T(8,128)S(1)}, f32[192,768]{1,0:T(8,128)}, u32[]{:S(2)}) copy-start(f32[192,768]{1,0:T(8,128)} %get-tuple-element.21) | copy-start | bytes 1769476

commit v2 on v1

--- a/solution.py
+++ b/solution.py
@@ -27,11 +27,11 @@
 
 def kernel(
     dims,
-    src, tgt, pool, rows_in, margin_col,
-    loss_out, sgrad, tgrad, pgrad,
+    src, tgt, pool, index_in, lang_in, margin_in,
+    loss_out, sg_out, tgrad, pgrad,
     tall, adj, prob, sel, want_send, want_recv, picks, slots_send, slots_recv, hp_send, hp_recv,
-    stats, sg_send, sg_recv, sib_send, sib_recv, rs_send, rs_recv,
-    t_ss, t_rs, fw_ss, w_ss, w_rs, p_ss, p_rs, s_ss, s_rs, h_ss, h_rs, st_ss, st_rs,
+    stats, line, mpad, sg_send, sg_recv, sib_send, sib_recv, rs_send, rs_recv,
+    t_ss, t_rs, up_ss, dn_ss, fu_ss, fd_ss, w_ss, w_rs, p_ss, p_rs, s_ss, s_rs, h_ss, h_rs, st_ss, st_rs,
     q_ss, q_rs, a_ss, a_rs, b_ss, b_rs, r_ss, r_rs,
 ):
     B, G, M, T, D, cap = dims
@@ -74,8 +74,14 @@
     for k in range(1, G):
         pl.semaphore_signal(barrier, inc=1, device_id={"grp": (g + k) % G}, device_id_type=MESH)
 
-    owner_row = rows_in[0:1, :]
-    loc_row = rows_in[1:2, :]
+    index_row = index_in[...]
+    owner_row = jnp.full((1, M), -1, jnp.int32)
+    loc_row = jnp.zeros((1, M), jnp.int32)
+    for j in range(B):
+        base = (g * B + j) * T
+        inside = (index_row >= base) & (index_row < base + T)
+        owner_row = jnp.where(inside, j, owner_row)
+        loc_row = jnp.where(inside, index_row - base, loc_row)
     present = owner_row >= 0
     col_id = lax.broadcasted_iota(jnp.int32, (T, M), 1)
     row_id = lax.broadcasted_iota(jnp.int32, (T, M), 0)
@@ -115,33 +121,66 @@
     cp = to_blk(tgt, tall.at[trows(b)], t_ss.at[0], t_rs.at[b], sib)
     cp.start()
     sends.append(cp)
-    for dz in range(1, Z):
-        cp = to_blk(tgt, tall.at[trows(b)], t_ss.at[dz], t_rs.at[b], blk_of(dz, c))
-        cp.start()
-        sends.append(cp)
+
+    def up_copy(block, step):
+        return to_blk(
+            tall.at[trows(block)], tall.at[trows(block)], up_ss.at[step], t_rs.at[block], b + 2
+        )
+
+    def down_copy(block, step):
+        return to_blk(
+            tall.at[trows(block)], tall.at[trows(block)], dn_ss.at[step], t_rs.at[block], b - 2
+        )
+
+    def side_copy(block, sems, step):
+        return to_blk(
+            tall.at[trows(block)], tall.at[trows(block)], sems.at[step], t_rs.at[block], sib
+        )
+
+    has_up = z + 1 < Z
+    has_down = z >= 1
     tall[trows(b), :] = tgt[...]
+
+    @pl.when(has_up)
+    def _():
+        up_copy(b, 0).start()
+
+    @pl.when(has_down)
+    def _():
+        down_copy(b, 0).start()
+
     want_recv[b] = want_send[b]
 
-    lang_id = lax.broadcasted_iota(jnp.int32, (margin_col.shape[0], M), 0)
-    margin_row = jnp.sum(
-        jnp.where(rows_in[2:3, :] == lang_id, margin_col[...], 0.0), axis=0, keepdims=True
-    )
+    mpad[...] = jnp.zeros_like(mpad)
+    mpad[0:1, 0 : margin_in.shape[1]] = margin_in[...]
+    m_all = mpad[0:1, :]
+    m_hi = m_all.astype(bf16).astype(f32)
+    m_mid = (m_all - m_hi).astype(bf16).astype(f32)
+    m_lo = m_all - m_hi - m_mid
+    m_id = lax.broadcasted_iota(jnp.int32, mpad.shape, 0)
+    m_parts = jnp.where(
+        m_id == 0, m_hi, jnp.where(m_id == 1, m_mid, jnp.where(m_id == 2, m_lo, 0.0))
+    ).astype(bf16)
+    lang_id = lax.broadcasted_iota(jnp.int32, (mpad.shape[1], M), 0)
+    lang_hot = jnp.where(lang_in[...] == lang_id, 1.0, 0.0).astype(bf16)
+    margin_row = jnp.sum(dot_nn(m_parts, lang_hot), axis=0, keepdims=True)
 
     def hit(j):
         return row_id - col_id == b * M - (g * B + j) * T
 
-    def score(j, carry):
-        top, pos = carry
+    line[0:1, :] = jnp.full((1, M), neg_fill, f32)
+    line[1:2, :] = jnp.zeros((1, M), f32)
+    line[2:3, :] = margin_row
+
+    def score(j):
         s = dot_nt(tall[trows(j), :], src[...])
         diag = hit(j)
-        s = s - jnp.where(diag, margin_row, 0.0)
+        s = s - jnp.where(diag, line[2:3, :], 0.0)
         adj[trows(j), :] = s
-        top = jnp.maximum(top, jnp.max(s, axis=0, keepdims=True))
-        pos = pos + jnp.sum(jnp.where(diag, s, 0.0), axis=0, keepdims=True)
-        return top, pos
-
-    carry = (jnp.full((1, M), neg_fill, f32), jnp.zeros((1, M), f32))
-    carry = score(b, carry)
+        line[0:1, :] = jnp.maximum(line[0:1, :], jnp.max(s, axis=0, keepdims=True))
+        line[1:2, :] += jnp.sum(jnp.where(diag, s, 0.0), axis=0, keepdims=True)
+
+    score(b)
 
     pool_id = lax.broadcasted_iota(jnp.int32, (T, cap), 0).astype(f32)
     for k in range(0, B):
@@ -162,30 +201,67 @@
         to_blk(tgt, tall.at[trows(j)], t_ss.at[0], t_rs.at[j], sib).wait_recv()
 
     wait_t(sib)
-    carry = score(sib, carry)
-    for dz in range(1, Z):
-        near = blk_of(dz, c)
-        wait_t(near)
-        cp = to_blk(tall.at[trows(near)], tall.at[trows(near)], fw_ss.at[dz], t_rs.at[near], sib)
-        cp.start()
-        sends.append(cp)
-        carry = score(near, carry)
+    score(sib)
+
+    def pass_on(step, carry):
+        below = z - 1 - step
+        above = z + 1 + step
+
+        @pl.when(below >= 0)
+        def _():
+            block = below * 2 + c
+            wait_t(block)
+
+            @pl.when(has_up)
+            def _():
+                up_copy(block, step + 1).start()
+
+            side_copy(block, fu_ss, step).start()
+
+        @pl.when(above < Z)
+        def _():
+            block = above * 2 + c
+            wait_t(block)
+
+            @pl.when(has_down)
+            def _():
+                down_copy(block, step + 1).start()
+
+            side_copy(block, fd_ss, step).start()
+
+        def use(q, inner):
+            at = jnp.where(q % 2 == 0, below, above)
+
+            @pl.when((at >= 0) & (at < Z))
+            def _():
+                far = q // 2
+                block = at * 2 + (c + far) % 2
+
+                @pl.when(far == 1)
+                def _():
+                    wait_t(block)
+
+                score(block)
+
+            return inner
+
+        lax.fori_loop(0, 4, use, 0)
+        return carry
+
     def fill_slots(j, carry):
         slots_send[j] = dot_nn(sel[crows(j), :], src[...]).astype(bf16)
         return carry
 
     lax.fori_loop(0, B, fill_slots, 0)
+    lax.fori_loop(0, Z - 1, pass_on, 0)
     for k in range(1, B):
         peer = (b + k) % B
         cp = to_blk(slots_send.at[peer], slots_recv.at[b], s_ss.at[k], s_rs.at[b], peer)
         cp.start()
         sends.append(cp)
     slots_recv[b] = slots_send[b]
-    for dz in range(1, Z):
-        far = blk_of(dz, 1 - c)
-        wait_t(far)
-        carry = score(far, carry)
-    top, pos = carry
+    top = line[0:1, :]
+    pos = line[1:2, :]
     for k in range(1, B):
         peer = (b + k) % B
         to_blk(picks.at[0], tall.at[frows(peer)], p_ss.at[0], p_rs.at[peer], peer).wait_recv()
@@ -266,6 +342,19 @@
 
     lax.fori_loop(0, B, fill_hard, 0)
 
+    V = W if N1 <= 2048 else W // 2
+    for n in range(M // V):
+        cols = pl.ds(n * V, V)
+        part = dot_tn(prob[:, cols], tall[...])
+        part = part + dot_tn(sel[:, cols], tall[pl.ds(N1, B * cap), :])
+        adj[pl.ds(n * V, V), 0:D] = part
+    for k in range(1, G):
+        peer = (g + k) % G
+        sg_send[k - 1] = adj[trows(peer), 0:D].astype(bf16)
+        cp = to_grp(sg_send.at[k - 1], sg_recv.at[k - 1], q_ss.at[k], q_rs.at[k], peer)
+        cp.start()
+        sends.append(cp)
+
     for dz in range(Z):
         j = blk_of(dz, 1 - c)
         sib_send[dz] = dot_nn(prob[trows(j), :], src[...]).astype(bf16)
@@ -284,19 +373,6 @@
             cp = to_blk(rs_send.at[dz - 1], rs_recv.at[dz - 1], r_ss.at[dz], r_rs.at[dz], j)
             cp.start()
             sends.append(cp)
-
-    V = W if N1 <= 2048 else W // 2
-    for n in range(M // V):
-        cols = pl.ds(n * V, V)
-        part = dot_tn(prob[:, cols], tall[...])
-        part = part + dot_tn(sel[:, cols], tall[pl.ds(N1, B * cap), :])
-        sgrad[pl.ds(n * V, V), :] = part
-    for k in range(1, G):
-        peer = (g + k) % G
-        sg_send[k - 1] = sgrad[trows(peer), :].astype(bf16)
-        cp = to_grp(sg_send.at[k - 1], sg_recv.at[k - 1], q_ss.at[k], q_rs.at[k], peer)
-        cp.start()
-        sends.append(cp)
 
     acc = jnp.zeros((T, D), f32)
     for k in range(0, B):
@@ -312,14 +388,14 @@
         acc = acc + dot_nn(jnp.where(hot, weight - hi, 0.0).astype(bf16), rows)
     pgrad[...] = acc
 
-    own = sgrad[trows(g), :]
+    own = adj[trows(g), 0:D]
     for k in range(1, G):
         to_grp(sg_send.at[0], sg_recv.at[k - 1], q_ss.at[0], q_rs.at[k], (g + k) % G).wait_recv()
         own = own + sg_recv[k - 1].astype(f32)
-    sgrad[trows(g), :] = own
+    sg_out[trows(g), :] = own.astype(bf16)
     for k in range(1, G):
         peer = (g + k) % G
-        cp = to_grp(sgrad.at[trows(g)], sgrad.at[trows(g)], a_ss.at[k], a_rs.at[g], peer)
+        cp = to_grp(sg_out.at[trows(g)], sg_out.at[trows(g)], a_ss.at[k], a_rs.at[g], peer)
         cp.start()
         sends.append(cp)
 
@@ -330,9 +406,45 @@
     tgrad[...] = final
     for k in range(1, G):
         peer = (g + k) % G
-        to_grp(sgrad.at[trows(g)], sgrad.at[trows(peer)], a_ss.at[0], a_rs.at[peer], peer).wait_recv()
+        to_grp(sg_out.at[trows(g)], sg_out.at[trows(peer)], a_ss.at[0], a_rs.at[peer], peer).wait_recv()
     for cp in sends:
         cp.wait_send()
+
+    @pl.when(has_up)
+    def _():
+        up_copy(b, 0).wait_send()
+
+    @pl.when(has_down)
+    def _():
+        down_copy(b, 0).wait_send()
+
+    def settle(step, carry):
+        below = z - 1 - step
+        above = z + 1 + step
+
+        @pl.when(below >= 0)
+        def _():
+            block = below * 2 + c
+
+            @pl.when(has_up)
+            def _():
+                up_copy(block, step + 1).wait_send()
+
+            side_copy(block, fu_ss, step).wait_send()
+
+        @pl.when(above < Z)
+        def _():
+            block = above * 2 + c
+
+            @pl.when(has_down)
+            def _():
+                down_copy(block, step + 1).wait_send()
+
+            side_copy(block, fd_ss, step).wait_send()
+
+        return carry
+
+    lax.fori_loop(0, Z - 1, settle, 0)
 
 
 def shards(source_emb, target_emb, hard_pool, hard_index, language, margin):
@@ -344,10 +456,7 @@
     per_block = max(2, (2 * T + owners - 1) // owners)
     cap = -(-(per_block * (M // T)) // 16) * 16
     Z = B // 2
-    g = lax.axis_index("grp")
-    owner = hard_index // T
-    local = jnp.where(owner // B == g, owner % B, -1)
-    rows_in = jnp.stack([local, hard_index % T, language])
+    LP = -(-margin.shape[0] // 128) * 128
     dims = (B, G, M, T, D, cap)
     dma = pltpu.SemaphoreType.DMA
     vmem = pl.BlockSpec(memory_space=pltpu.VMEM)
@@ -357,11 +466,11 @@
         functools.partial(kernel, dims),
         out_shape=[
             jax.ShapeDtypeStruct((1, M), f32),
-            jax.ShapeDtypeStruct((M, D), f32),
+            jax.ShapeDtypeStruct((M, D), bf16),
             jax.ShapeDtypeStruct((T, D), f32),
             jax.ShapeDtypeStruct((T, D), f32),
         ],
-        in_specs=[vmem] * 5,
+        in_specs=[vmem] * 6,
         out_specs=[vmem] * 4,
         scratch_shapes=[
             pltpu.VMEM((K, D), bf16),
@@ -376,13 +485,15 @@
             pltpu.VMEM((B, 8, 128), f32),
             pltpu.VMEM((B, 8, 128), f32),
             pltpu.VMEM((G, 8, M), f32),
+            pltpu.VMEM((8, M), f32),
+            pltpu.VMEM((8, LP), f32),
             pltpu.VMEM((G - 1, T, D), bf16),
             pltpu.VMEM((G - 1, T, D), bf16),
             pltpu.VMEM((Z, T, D), bf16),
             pltpu.VMEM((Z, T, D), bf16),
             pltpu.VMEM((Z - 1, T, D), bf16),
             pltpu.VMEM((Z - 1, T, D), bf16),
-            dma((Z,)), dma((B,)), dma((Z,)),
+            dma((1,)), dma((B,)), dma((Z,)), dma((Z,)), dma((Z,)), dma((Z,)),
             dma((B,)), dma((B,)), dma((B,)), dma((B,)),
             dma((B,)), dma((B,)), dma((B,)), dma((B,)),
             dma((G,)), dma((G,)),
@@ -397,10 +508,10 @@
         ),
         name="loss_kernel",
     )(
-        source_emb, target_emb, hard_pool, rows_in,
-        margin.reshape(margin.shape[0], 1),
+        source_emb, target_emb, hard_pool, hard_index.reshape(1, M), language.reshape(1, M),
+        margin.reshape(1, margin.shape[0]),
     )
-    return loss.reshape(M), sg, tg, pg
+    return loss.reshape(M), sg.astype(f32), tg, pg
 
 
 def solution(mesh):

time: 125 us -> 103 us (0.82)
  the two profiles are of different devices: /device:TPU:24 before, /device:TPU:0 now
where the time goes in v2:
time: 103 us
  Pallas kernels  94.4 us (92%)
  local copies, waits for them, and re-layouts  4.18 us (4%)
  other arithmetic  3.51 us (3%)
    pallas_call x1, Pallas kernels, shards(): pl.pallas_call(functools.partial(kernel, dims), out_shape=[jax.ShapeDtype...  94.4 us
    convert_element_type x1, other arithmetic, shards(): return (loss.reshape(M), sg.astype(f32), tg, pg)  2.91 us

profile of v2, /device:TPU:0, one launch (start us, length us, event | category | flops | bytes accessed | tf_op | source)
XLA Modules:
  0.0 102.8 jit_solution(13901298584498807349)
XLA Ops:
  0.6 1.3 %reshape.20.index_in = s32[1,768]{1,0:T(1,128)} reshape(s32[768]{0:T(1024)} %param.9) | data formatting | bytes 6144 | tf_op jit(solution)/shard_map/reshape | solution.py:511
  1.9 1.3 %reshape.21.lang_in = s32[1,768]{1,0:T(1,128)} reshape(s32[768]{0:T(1024)} %param.10) | data formatting | bytes 6144 | tf_op jit(solution)/shard_map/reshape | solution.py:511
  3.2 94.4 %loss_kernel.1 = (f32[1,768]{1,0:T(1,128)}, bf16[768,768]{1,0:T(8,128)(2,1)}, f32[192,768]{1,0:T(8,128)}, f32[192,768]{1,0:T(8,128)}) custom-call(bf16[768,768]{1,0:T(8,128)(2,1)} %src.1, bf16[192,768]{1,0:T(8,128)(2,1)} %tgt.1, bf16[192,768]{1,0:T(8,128)(2,1)} %pool.1, s32[1,768]{1,0:T(1,128)} %reshape.20.index_in, s32[1,768]{1,0:T(1,128)} %reshape.21.lang_in, ...), custom_call_target="tpu_custom_call" | custom-call | flops 7247757312 | bytes 4718592 | tf_op jit(solution)/shard_map/loss_kernel/pallas_call | solution.py:465
  97.6 0.0 copy-start.2
  97.6 0.0 copy-start.1
  97.6 2.9 %convert_element_type.3 = f32[768,768]{1,0:T(8,128)} convert(bf16[768,768]{1,0:T(8,128)(2,1)} %get-tuple-element.9) | non-fusion elementwise | flops 589824 | bytes 3538944 | tf_op jit(solution)/shard_map/convert_element_type | solution.py:514
  100.5 0.0 copy-start
  100.5 0.0 copy-done.2
  100.5 0.6 reduce
  101.1 0.0 copy-done.1
  101.1 0.8 copy.12
  101.9 0.0 copy-done
  101.9 0.8 copy.13
Async XLA Ops:
  97.6 2.9 %copy-start.2 = (f32[1,768]{1,0:T(1,128)S(1)}, f32[1,768]{1,0:T(1,128)}, u32[]{:S(2)}) copy-start(f32[1,768]{1,0:T(1,128)} %get-tuple-element.8) | copy-start | bytes 9220
  97.6 3.5 %copy-start.1 = (f32[192,768]{1,0:T(8,128)S(1)}, f32[192,768]{1,0:T(8,128)}, u32[]{:S(2)}) copy-start(f32[192,768]{1,0:T(8,128)} %get-tuple-element.18) | copy-start | bytes 1769476
  100.5 1.4 %copy-start = (f32[192,768]{1,0:T(8,128)S(1)}, f32[192,768]{1,0:T(8,128)}, u32[]{:S(2)}) copy-start(f32[192,768]{1,0:T(8,128)} %get-tuple-element.19) | copy-start | bytes 1769476

commit v3 on v2

--- a/solution.py
+++ b/solution.py
@@ -28,11 +28,11 @@
 def kernel(
     dims,
     src, tgt, pool, index_in, lang_in, margin_in,
-    loss_out, sg_out, tgrad, pgrad,
+    loss_out, sg_out, sg_scale, tgrad, pgrad,
     tall, adj, prob, sel, want_send, want_recv, picks, slots_send, slots_recv, hp_send, hp_recv,
-    stats, line, mpad, sg_send, sg_recv, sib_send, sib_recv, rs_send, rs_recv,
+    stats, part_stats, line, mpad, sg_send, sg_recv, sib_send, sib_recv, rs_send, rs_recv,
     t_ss, t_rs, up_ss, dn_ss, fu_ss, fd_ss, w_ss, w_rs, p_ss, p_rs, s_ss, s_rs, h_ss, h_rs, st_ss, st_rs,
-    q_ss, q_rs, a_ss, a_rs, b_ss, b_rs, r_ss, r_rs,
+    q_ss, q_rs, a_ss, a_rs, c_ss, c_rs, b_ss, b_rs, r_ss, r_rs,
 ):
     B, G, M, T, D, cap = dims
     Z = B // 2
@@ -68,13 +68,51 @@
             device_id={"grp": peer}, device_id_type=MESH,
         )
 
+    def one_row(ref):
+        return jnp.concatenate([ref[i : i + 1, :] for i in range(M // 128)], axis=1)
+
     barrier = pltpu.get_barrier_semaphore()
     for k in range(1, B):
         pl.semaphore_signal(barrier, inc=1, device_id={"blk": (b + k) % B}, device_id_type=MESH)
     for k in range(1, G):
         pl.semaphore_signal(barrier, inc=1, device_id={"grp": (g + k) % G}, device_id_type=MESH)
 
-    index_row = index_in[...]
+    pl.semaphore_wait(barrier, B - 1 + G - 1)
+
+    sends = []
+    cp = to_blk(tgt, tall.at[trows(b)], t_ss.at[0], t_rs.at[b], sib)
+    cp.start()
+    sends.append(cp)
+
+    def up_copy(block, step):
+        return to_blk(
+            tall.at[trows(block)], tall.at[trows(block)], up_ss.at[step], t_rs.at[block], b + 2
+        )
+
+    def down_copy(block, step):
+        return to_blk(
+            tall.at[trows(block)], tall.at[trows(block)], dn_ss.at[step], t_rs.at[block], b - 2
+        )
+
+    def side_copy(block, sems, step):
+        return to_blk(
+            tall.at[trows(block)], tall.at[trows(block)], sems.at[step], t_rs.at[block], sib
+        )
+
+    has_up = z + 1 < Z
+    has_down = z >= 1
+    tall[trows(b), :] = tgt[...]
+
+    @pl.when(has_up)
+    def _():
+        up_copy(b, 0).start()
+
+    @pl.when(has_down)
+    def _():
+        down_copy(b, 0).start()
+
+
+    index_row = one_row(index_in)
     owner_row = jnp.full((1, M), -1, jnp.int32)
     loc_row = jnp.zeros((1, M), jnp.int32)
     for j in range(B):
@@ -110,45 +148,11 @@
 
     lax.fori_loop(0, B, fill_sel, 0)
 
-    pl.semaphore_wait(barrier, B - 1 + G - 1)
-
-    sends = []
     for k in range(1, B):
         peer = (b + k) % B
         cp = to_blk(want_send.at[peer], want_recv.at[b], w_ss.at[k], w_rs.at[b], peer)
         cp.start()
         sends.append(cp)
-    cp = to_blk(tgt, tall.at[trows(b)], t_ss.at[0], t_rs.at[b], sib)
-    cp.start()
-    sends.append(cp)
-
-    def up_copy(block, step):
-        return to_blk(
-            tall.at[trows(block)], tall.at[trows(block)], up_ss.at[step], t_rs.at[block], b + 2
-        )
-
-    def down_copy(block, step):
-        return to_blk(
-            tall.at[trows(block)], tall.at[trows(block)], dn_ss.at[step], t_rs.at[block], b - 2
-        )
-
-    def side_copy(block, sems, step):
-        return to_blk(
-            tall.at[trows(block)], tall.at[trows(block)], sems.at[step], t_rs.at[block], sib
-        )
-
-    has_up = z + 1 < Z
-    has_down = z >= 1
-    tall[trows(b), :] = tgt[...]
-
-    @pl.when(has_up)
-    def _():
-        up_copy(b, 0).start()
-
-    @pl.when(has_down)
-    def _():
-        down_copy(b, 0).start()
-
     want_recv[b] = want_send[b]
 
     mpad[...] = jnp.zeros_like(mpad)
@@ -162,13 +166,12 @@
         m_id == 0, m_hi, jnp.where(m_id == 1, m_mid, jnp.where(m_id == 2, m_lo, 0.0))
     ).astype(bf16)
     lang_id = lax.broadcasted_iota(jnp.int32, (mpad.shape[1], M), 0)
-    lang_hot = jnp.where(lang_in[...] == lang_id, 1.0, 0.0).astype(bf16)
+    lang_hot = jnp.where(one_row(lang_in) == lang_id, 1.0, 0.0).astype(bf16)
     margin_row = jnp.sum(dot_nn(m_parts, lang_hot), axis=0, keepdims=True)
 
     def hit(j):
         return row_id - col_id == b * M - (g * B + j) * T
 
-    line[0:1, :] = jnp.full((1, M), neg_fill, f32)
     line[1:2, :] = jnp.zeros((1, M), f32)
     line[2:3, :] = margin_row
 
@@ -176,8 +179,11 @@
         s = dot_nt(tall[trows(j), :], src[...])
         diag = hit(j)
         s = s - jnp.where(diag, line[2:3, :], 0.0)
-        adj[trows(j), :] = s
-        line[0:1, :] = jnp.maximum(line[0:1, :], jnp.max(s, axis=0, keepdims=True))
+        own_top = jnp.max(s, axis=0, keepdims=True)
+        e = jnp.exp(s - own_top)
+        adj[trows(j), :] = e
+        part_stats[j, 0:1, :] = own_top
+        part_stats[j, 1:2, :] = jnp.sum(e, axis=0, keepdims=True)
         line[1:2, :] += jnp.sum(jnp.where(diag, s, 0.0), axis=0, keepdims=True)
 
     score(b)
@@ -260,7 +266,6 @@
         cp.start()
         sends.append(cp)
     slots_recv[b] = slots_send[b]
-    top = line[0:1, :]
     pos = line[1:2, :]
     for k in range(1, B):
         peer = (b + k) % B
@@ -272,13 +277,13 @@
 
     hard = lax.fori_loop(0, B, hard_part, jnp.zeros((1, M), f32))
     hard = jnp.where(present, hard, neg_fill)
-    top = jnp.maximum(top, hard)
-
-    def add_exp(j, acc):
-        return acc + jnp.sum(jnp.exp(adj[trows(j), :] - top), axis=0, keepdims=True)
+    top = hard
+    for j in range(B):
+        top = jnp.maximum(top, part_stats[j, 0:1, :])
 
     total = jnp.where(present, jnp.exp(hard - top), 0.0)
-    total = lax.fori_loop(0, B, add_exp, total)
+    for j in range(B):
+        total = total + part_stats[j, 1:2, :] * jnp.exp(part_stats[j, 0:1, :] - top)
     stats[g, 0:1, :] = top
     stats[g, 1:2, :] = total
     stats[g, 2:3, :] = pos
@@ -299,8 +304,37 @@
         all_total = all_total + stats[q, 1:2, :] * jnp.exp(stats[q, 0:1, :] - all_top)
         all_pos = all_pos + stats[q, 2:3, :]
     log_total = all_top + jnp.log(all_total)
-    loss_out[...] = log_total - all_pos
+    loss = log_total - all_pos
+    for i in range(M // 128):
+        loss_out[i : i + 1, :] = loss[:, i * 128 : (i + 1) * 128]
     hard_prob = jnp.where(present, jnp.exp(hard - log_total), 0.0)
+
+    def make_prob(j, carry):
+        scale = jnp.exp(part_stats[j, 0:1, :] - log_total)
+        p = adj[trows(j), :] * scale - jnp.where(hit(j), 1.0, 0.0)
+        prob[trows(j), :] = p.astype(bf16)
+        return carry
+
+    lax.fori_loop(0, B, make_prob, 0)
+
+    for dz in range(Z):
+        j = blk_of(dz, 1 - c)
+        sib_send[dz] = dot_nn(prob[trows(j), :], src[...]).astype(bf16)
+        cp = to_blk(sib_send.at[dz], sib_recv.at[dz], b_ss.at[dz], b_rs.at[dz], sib)
+        cp.start()
+        sends.append(cp)
+    for dz in list(range(1, Z)) + [0]:
+        j = blk_of(dz, c)
+        term = dot_nn(prob[trows(j), :], src[...])
+        to_blk(sib_send.at[0], sib_recv.at[dz], b_ss.at[0], b_rs.at[dz], sib).wait_recv()
+        term = term + sib_recv[dz].astype(f32)
+        if dz == 0:
+            tgrad[...] = term
+        else:
+            rs_send[dz - 1] = term.astype(bf16)
+            cp = to_blk(rs_send.at[dz - 1], rs_recv.at[dz - 1], r_ss.at[dz], r_rs.at[dz], j)
+            cp.start()
+            sends.append(cp)
 
     hp_hi = hard_prob.astype(bf16)
     rest = hard_prob - hp_hi.astype(f32)
@@ -327,13 +361,6 @@
         sends.append(cp)
     hp_recv[b] = hp_send[b]
 
-    def make_prob(j, carry):
-        p = jnp.exp(adj[trows(j), :] - log_total) - jnp.where(hit(j), 1.0, 0.0)
-        prob[trows(j), :] = p.astype(bf16)
-        return carry
-
-    lax.fori_loop(0, B, make_prob, 0)
-
     def fill_hard(j, carry):
         hot = sel[crows(j), :].astype(f32)
         prob[frows(j), :] = (hot * hp_hi.astype(f32)).astype(bf16)
@@ -354,25 +381,6 @@
         cp = to_grp(sg_send.at[k - 1], sg_recv.at[k - 1], q_ss.at[k], q_rs.at[k], peer)
         cp.start()
         sends.append(cp)
-
-    for dz in range(Z):
-        j = blk_of(dz, 1 - c)
-        sib_send[dz] = dot_nn(prob[trows(j), :], src[...]).astype(bf16)
-        cp = to_blk(sib_send.at[dz], sib_recv.at[dz], b_ss.at[dz], b_rs.at[dz], sib)
-        cp.start()
-        sends.append(cp)
-    for dz in list(range(1, Z)) + [0]:
-        j = blk_of(dz, c)
-        term = dot_nn(prob[trows(j), :], src[...])
-        to_blk(sib_send.at[0], sib_recv.at[dz], b_ss.at[0], b_rs.at[dz], sib).wait_recv()
-        term = term + sib_recv[dz].astype(f32)
-        if dz == 0:
-            tgrad[...] = term
-        else:
-            rs_send[dz - 1] = term.astype(bf16)
-            cp = to_blk(rs_send.at[dz - 1], rs_recv.at[dz - 1], r_ss.at[dz], r_rs.at[dz], j)
-            cp.start()
-            sends.append(cp)
 
     acc = jnp.zeros((T, D), f32)
     for k in range(0, B):
@@ -392,10 +400,16 @@
     for k in range(1, G):
         to_grp(sg_send.at[0], sg_recv.at[k - 1], q_ss.at[0], q_rs.at[k], (g + k) % G).wait_recv()
         own = own + sg_recv[k - 1].astype(f32)
-    sg_out[trows(g), :] = own.astype(bf16)
+    limit = jnp.maximum(jnp.max(jnp.abs(own), axis=0, keepdims=True), 1e-30)
+    coded = jnp.floor(own * (32767.0 / limit) + 0.5)
+    sg_out[trows(g), :] = coded.astype(jnp.int32).astype(jnp.int16)
+    sg_scale[g] = jnp.broadcast_to(limit * (1.0 / 32767.0), (8, D))
     for k in range(1, G):
         peer = (g + k) % G
         cp = to_grp(sg_out.at[trows(g)], sg_out.at[trows(g)], a_ss.at[k], a_rs.at[g], peer)
+        cp.start()
+        sends.append(cp)
+        cp = to_grp(sg_scale.at[g], sg_scale.at[g], c_ss.at[k], c_rs.at[g], peer)
         cp.start()
         sends.append(cp)
 
@@ -407,6 +421,7 @@
     for k in range(1, G):
         peer = (g + k) % G
         to_grp(sg_out.at[trows(g)], sg_out.at[trows(peer)], a_ss.at[0], a_rs.at[peer], peer).wait_recv()
+        to_grp(sg_scale.at[g], sg_scale.at[peer], c_ss.at[0], c_rs.at[peer], peer).wait_recv()
     for cp in sends:
         cp.wait_send()
 
@@ -462,16 +477,17 @@
     vmem = pl.BlockSpec(memory_space=pltpu.VMEM)
     K = B * T + B * cap
     flops = 2 * M * D * (3 * B * T + 4 * B * cap)
-    loss, sg, tg, pg = pl.pallas_call(
+    loss, coded, scale, tg, pg = pl.pallas_call(
         functools.partial(kernel, dims),
         out_shape=[
-            jax.ShapeDtypeStruct((1, M), f32),
-            jax.ShapeDtypeStruct((M, D), bf16),
+            jax.ShapeDtypeStruct((M // 128, 128), f32),
+            jax.ShapeDtypeStruct((M, D), jnp.int16),
+            jax.ShapeDtypeStruct((G, 8, D), f32),
             jax.ShapeDtypeStruct((T, D), f32),
             jax.ShapeDtypeStruct((T, D), f32),
         ],
         in_specs=[vmem] * 6,
-        out_specs=[vmem] * 4,
+        out_specs=[vmem] * 5,
         scratch_shapes=[
             pltpu.VMEM((K, D), bf16),
             pltpu.VMEM((B * T, M), f32),
@@ -485,6 +501,7 @@
             pltpu.VMEM((B, 8, 128), f32),
             pltpu.VMEM((B, 8, 128), f32),
             pltpu.VMEM((G, 8, M), f32),
+            pltpu.VMEM((B, 8, M), f32),
             pltpu.VMEM((8, M), f32),
             pltpu.VMEM((8, LP), f32),
             pltpu.VMEM((G - 1, T, D), bf16),
@@ -497,7 +514,7 @@
             dma((B,)), dma((B,)), dma((B,)), dma((B,)),
             dma((B,)), dma((B,)), dma((B,)), dma((B,)),
             dma((G,)), dma((G,)),
-            dma((G,)), dma((G,)), dma((G,)), dma((G,)),
+            dma((G,)), dma((G,)), dma((G,)), dma((G,)), dma((G,)), dma((G,)),
             dma((Z,)), dma((Z,)), dma((Z,)), dma((Z,)),
         ],
         compiler_params=pltpu.CompilerParams(
@@ -508,10 +525,11 @@
         ),
         name="loss_kernel",
     )(
-        source_emb, target_emb, hard_pool, hard_index.reshape(1, M), language.reshape(1, M),
+        source_emb, target_emb, hard_pool, hard_index.reshape(M // 128, 128), language.reshape(M // 128, 128),
         margin.reshape(1, margin.shape[0]),
     )
-    return loss.reshape(M), sg.astype(f32), tg, pg
+    sg = (coded.reshape(G, T, D).astype(f32) * scale[:, 0:1, :]).reshape(M, D)
+    return loss.reshape(M), sg, tg, pg
 
 
 def solution(mesh):

time: 103 us -> 111 us (1.078)
  Pallas kernels: 94.4 us -> 104 us
    pallas_call x1, Pallas kernels: 94.4 us -> 104 us  [shards(): pl.pallas_call(functools.partial(kernel, dims), out_shape=[jax.ShapeDtype...]
    mul x0 -> x1, other arithmetic: none -> 3.12 us  [shards(): sg = (coded.reshape(G, T, D).astype(f32) * scale[:, 0:1, :]).reshape(M, D)]
    convert_element_type x1 -> x0, other arithmetic: 2.91 us -> none  [shards(): return (loss.reshape(M), sg.astype(f32), tg, pg)]
    reshape x2 -> x0, local copies, waits for them, and re-layouts: 2.53 us -> none  [the longest x1 1.27 us: shards(): hard_index.reshape(1, M)]
    unnamed x8 -> x10, local copies, waits for them, and re-layouts: 1.64 us -> 2.24 us
where the time goes in v3:
time: 111 us
  Pallas kernels  104 us (94%)
  local copies, waits for them, and re-layouts  3.2 us (3%)
  other arithmetic  3.12 us (3%)
    pallas_call x1, Pallas kernels, shards(): pl.pallas_call(functools.partial(kernel, dims), out_shape=[jax.ShapeDtype...  104 us
    mul x1, other arithmetic, shards(): sg = (coded.reshape(G, T, D).astype(f32) * scale[:, 0:1, :]).reshape(M, D)  3.12 us
    unnamed x10, local copies, waits for them, and re-layouts  2.24 us

profile of v3, /device:TPU:0, one launch (start us, length us, event | category | flops | bytes accessed | tf_op | source)
XLA Modules:
  0.0 110.7 jit_solution(13732989334402536442)
XLA Ops:
  0.6 103.8 %loss_kernel.1 = (f32[6,128]{1,0:T(8,128)}, s16[768,768]{1,0:T(8,128)(2,1)}, f32[4,8,768]{2,1,0:T(8,128)}, f32[192,768]{1,0:T(8,128)}, f32[192,768]{1,0:T(8,128)}) custom-call(bf16[768,768]{1,0:T(8,128)(2,1)} %src.1, bf16[192,768]{1,0:T(8,128)(2,1)} %tgt.1, bf16[192,768]{1,0:T(8,128)(2,1)} %pool.1, s32[6,128]{1,0:T(8,128)} %bitcast.11, s32[6,128]{1,0:T(8,128)} %bitcast.12, ...), custom_call_target="tpu_custom_call" | custom-call | flops 7247757312 | bytes 4718592 | tf_op jit(solution)/shard_map/loss_kernel/pallas_call | solution.py:480
  104.4 0.0 copy-start.2
  104.4 0.0 copy-start.1
  104.4 1.0 slice.3
  105.4 0.0 copy-start
  105.4 3.1 %bitcast_multiply_fusion = f32[768,768]{1,0:T(8,128)} fusion(s16[768,768]{1,0:T(8,128)(2,1)} %get-tuple-element.10, f32[4,768]{1,0:T(4,128)S(1)} %bitcast.9), kind=kLoop, calls=%fused_computation | loop fusion | flops 1179648 | bytes 3551232 | tf_op jit(solution)/shard_map/mul | solution.py:531
  108.5 0.0 copy-done.2
  108.5 0.6 copy.16
  109.1 0.0 copy-done.1
  109.1 0.8 copy.17
  109.9 0.0 copy-done
  109.9 0.8 copy.18
  (1 shorter events, 0.0 us)
Async XLA Ops:
  104.4 4.1 %copy-start.2 = (f32[6,128]{1,0:T(8,128)S(1)}, f32[6,128]{1,0:T(8,128)}, u32[]{:S(2)}) copy-start(f32[6,128]{1,0:T(8,128)} %get-tuple-element.9) | copy-start | bytes 9220
  104.4 4.7 %copy-start.1 = (f32[192,768]{1,0:T(8,128)S(1)}, f32[192,768]{1,0:T(8,128)}, u32[]{:S(2)}) copy-start(f32[192,768]{1,0:T(8,128)} %get-tuple-element.20) | copy-start | bytes 1769476
  105.4 4.5 %copy-start = (f32[192,768]{1,0:T(8,128)S(1)}, f32[192,768]{1,0:T(8,128)}, u32[]{:S(2)}) copy-start(f32[192,768]{1,0:T(8,128)} %get-tuple-element.21) | copy-start | bytes 1769476

commit v4 on v3

--- a/solution.py
+++ b/solution.py
@@ -260,12 +260,6 @@
 
     lax.fori_loop(0, B, fill_slots, 0)
     lax.fori_loop(0, Z - 1, pass_on, 0)
-    for k in range(1, B):
-        peer = (b + k) % B
-        cp = to_blk(slots_send.at[peer], slots_recv.at[b], s_ss.at[k], s_rs.at[b], peer)
-        cp.start()
-        sends.append(cp)
-    slots_recv[b] = slots_send[b]
     pos = line[1:2, :]
     for k in range(1, B):
         peer = (b + k) % B
@@ -292,6 +286,12 @@
         cp = to_grp(stats.at[g], stats.at[g], st_ss.at[k], st_rs.at[g], peer)
         cp.start()
         sends.append(cp)
+    for k in range(1, B):
+        peer = (b + k) % B
+        cp = to_blk(slots_send.at[peer], slots_recv.at[b], s_ss.at[k], s_rs.at[b], peer)
+        cp.start()
+        sends.append(cp)
+    slots_recv[b] = slots_send[b]
     for k in range(1, G):
         peer = (g + k) % G
         to_grp(stats.at[g], stats.at[peer], st_ss.at[0], st_rs.at[peer], peer).wait_recv()
@@ -309,6 +309,31 @@
         loss_out[i : i + 1, :] = loss[:, i * 128 : (i + 1) * 128]
     hard_prob = jnp.where(present, jnp.exp(hard - log_total), 0.0)
 
+    hp_hi = hard_prob.astype(bf16)
+    rest = hard_prob - hp_hi.astype(f32)
+    hp_mid = rest.astype(bf16)
+    hp_lo = (rest - hp_mid.astype(f32)).astype(bf16)
+    part_id = lax.broadcasted_iota(jnp.int32, (8, M), 0)
+    hp8 = jnp.where(
+        part_id == 0,
+        hp_hi.astype(f32),
+        jnp.where(
+            part_id == 1, hp_mid.astype(f32), jnp.where(part_id == 2, hp_lo.astype(f32), 0.0)
+        ),
+    ).astype(bf16)
+
+    def fill_hp(j, carry):
+        hp_send[j, :, 0:cap] = dot_nt(hp8, sel[crows(j), :])
+        return carry
+
+    lax.fori_loop(0, B, fill_hp, 0)
+    for k in range(1, B):
+        peer = (b + k) % B
+        cp = to_blk(hp_send.at[peer], hp_recv.at[b], h_ss.at[k], h_rs.at[b], peer)
+        cp.start()
+        sends.append(cp)
+    hp_recv[b] = hp_send[b]
+
     def make_prob(j, carry):
         scale = jnp.exp(part_stats[j, 0:1, :] - log_total)
         p = adj[trows(j), :] * scale - jnp.where(hit(j), 1.0, 0.0)
@@ -316,6 +341,27 @@
         return carry
 
     lax.fori_loop(0, B, make_prob, 0)
+
+    def fill_hard(j, carry):
+        hot = sel[crows(j), :].astype(f32)
+        prob[frows(j), :] = (hot * hp_hi.astype(f32)).astype(bf16)
+        sel[crows(j), :] = (hot * hp_mid.astype(f32)).astype(bf16)
+        return carry
+
+    lax.fori_loop(0, B, fill_hard, 0)
+
+    V = W if N1 <= 2048 else W // 2
+    for n in range(M // V):
+        cols = pl.ds(n * V, V)
+        part = dot_tn(prob[:, cols], tall[...])
+        part = part + dot_tn(sel[:, cols], tall[pl.ds(N1, B * cap), :])
+        adj[pl.ds(n * V, V), 0:D] = part
+    for k in range(1, G):
+        peer = (g + k) % G
+        sg_send[k - 1] = adj[trows(peer), 0:D].astype(bf16)
+        cp = to_grp(sg_send.at[k - 1], sg_recv.at[k - 1], q_ss.at[k], q_rs.at[k], peer)
+        cp.start()
+        sends.append(cp)
 
     for dz in range(Z):
         j = blk_of(dz, 1 - c)
@@ -336,49 +382,20 @@
             cp.start()
             sends.append(cp)
 
-    hp_hi = hard_prob.astype(bf16)
-    rest = hard_prob - hp_hi.astype(f32)
-    hp_mid = rest.astype(bf16)
-    hp_lo = (rest - hp_mid.astype(f32)).astype(bf16)
-    part_id = lax.broadcasted_iota(jnp.int32, (8, M), 0)
-    hp8 = jnp.where(
-        part_id == 0,
-        hp_hi.astype(f32),
-        jnp.where(
-            part_id == 1, hp_mid.astype(f32), jnp.where(part_id == 2, hp_lo.astype(f32), 0.0)
-        ),
-    ).astype(bf16)
-
-    def fill_hp(j, carry):
-        hp_send[j, :, 0:cap] = dot_nt(hp8, sel[crows(j), :])
-        return carry
-
-    lax.fori_loop(0, B, fill_hp, 0)
-    for k in range(1, B):
-        peer = (b + k) % B
-        cp = to_blk(hp_send.at[peer], hp_recv.at[b], h_ss.at[k], h_rs.at[b], peer)
-        cp.start()
-        sends.append(cp)
-    hp_recv[b] = hp_send[b]
-
-    def fill_hard(j, carry):
-        hot = sel[crows(j), :].astype(f32)
-        prob[frows(j), :] = (hot * hp_hi.astype(f32)).astype(bf16)
-        sel[crows(j), :] = (hot * hp_mid.astype(f32)).astype(bf16)
-        return carry
-
-    lax.fori_loop(0, B, fill_hard, 0)
-
-    V = W if N1 <= 2048 else W // 2
-    for n in range(M // V):
-        cols = pl.ds(n * V, V)
-        part = dot_tn(prob[:, cols], tall[...])
-        part = part + dot_tn(sel[:, cols], tall[pl.ds(N1, B * cap), :])
-        adj[pl.ds(n * V, V), 0:D] = part
+    own = adj[trows(g), 0:D]
+    for k in range(1, G):
+        to_grp(sg_send.at[0], sg_recv.at[k - 1], q_ss.at[0], q_rs.at[k], (g + k) % G).wait_recv()
+        own = own + sg_recv[k - 1].astype(f32)
+    limit = jnp.maximum(jnp.max(jnp.abs(own), axis=0, keepdims=True), 1e-30)
+    coded = jnp.floor(own * (32767.0 / limit) + 0.5)
+    sg_out[trows(g), :] = coded.astype(jnp.int32).astype(jnp.int16)
+    sg_scale[g] = jnp.broadcast_to(limit * (1.0 / 32767.0), (8, D))
     for k in range(1, G):
         peer = (g + k) % G
-        sg_send[k - 1] = adj[trows(peer), 0:D].astype(bf16)
-        cp = to_grp(sg_send.at[k - 1], sg_recv.at[k - 1], q_ss.at[k], q_rs.at[k], peer)
+        cp = to_grp(sg_out.at[trows(g)], sg_out.at[trows(g)], a_ss.at[k], a_rs.at[g], peer)
+        cp.start()
+        sends.append(cp)
+        cp = to_grp(sg_scale.at[g], sg_scale.at[g], c_ss.at[k], c_rs.at[g], peer)
         cp.start()
         sends.append(cp)
 
@@ -395,23 +412,6 @@
         acc = acc + dot_nn(jnp.where(hot, hi, 0.0).astype(bf16), rows)
         acc = acc + dot_nn(jnp.where(hot, weight - hi, 0.0).astype(bf16), rows)
     pgrad[...] = acc
-
-    own = adj[trows(g), 0:D]
-    for k in range(1, G):
-        to_grp(sg_send.at[0], sg_recv.at[k - 1], q_ss.at[0], q_rs.at[k], (g + k) % G).wait_recv()
-        own = own + sg_recv[k - 1].astype(f32)
-    limit = jnp.maximum(jnp.max(jnp.abs(own), axis=0, keepdims=True), 1e-30)
-    coded = jnp.floor(own * (32767.0 / limit) + 0.5)
-    sg_out[trows(g), :] = coded.astype(jnp.int32).astype(jnp.int16)
-    sg_scale[g] = jnp.broadcast_to(limit * (1.0 / 32767.0), (8, D))
-    for k in range(1, G):
-        peer = (g + k) % G
-        cp = to_grp(sg_out.at[trows(g)], sg_out.at[trows(g)], a_ss.at[k], a_rs.at[g], peer)
-        cp.start()
-        sends.append(cp)
-        cp = to_grp(sg_scale.at[g], sg_scale.at[g], c_ss.at[k], c_rs.at[g], peer)
-        cp.start()
-        sends.append(cp)
 
     final = tgrad[...]
     for dz in range(1, Z):

time: 111 us -> 104 us (0.937)
  Pallas kernels: 104 us -> 97 us
    pallas_call x1, Pallas kernels: 104 us -> 97 us  [shards(): pl.pallas_call(functools.partial(kernel, dims), out_shape=[jax.ShapeDtype...]
where the time goes in v4:
time: 104 us
  Pallas kernels  97 us (93%)
  local copies, waits for them, and re-layouts  3.2 us (3%)
  other arithmetic  3.12 us (3%)
    pallas_call x1, Pallas kernels, shards(): pl.pallas_call(functools.partial(kernel, dims), out_shape=[jax.ShapeDtype...  97 us
    mul x1, other arithmetic, shards(): sg = (coded.reshape(G, T, D).astype(f32) * scale[:, 0:1, :]).reshape(M, D)  3.12 us
    unnamed x10, local copies, waits for them, and re-layouts  2.24 us

profile of v4, /device:TPU:0, one launch (start us, length us, event | category | flops | bytes accessed | tf_op | source)
XLA Modules:
  0.0 104.0 jit_solution(3861658736643605842)
XLA Ops:
  0.6 97.0 %loss_kernel.1 = (f32[6,128]{1,0:T(8,128)}, s16[768,768]{1,0:T(8,128)(2,1)}, f32[4,8,768]{2,1,0:T(8,128)}, f32[192,768]{1,0:T(8,128)}, f32[192,768]{1,0:T(8,128)}) custom-call(bf16[768,768]{1,0:T(8,128)(2,1)} %src.1, bf16[192,768]{1,0:T(8,128)(2,1)} %tgt.1, bf16[192,768]{1,0:T(8,128)(2,1)} %pool.1, s32[6,128]{1,0:T(8,128)} %bitcast.11, s32[6,128]{1,0:T(8,128)} %bitcast.12, ...), custom_call_target="tpu_custom_call" | custom-call | flops 7247757312 | bytes 4718592 | tf_op jit(solution)/shard_map/loss_kernel/pallas_call | solution.py:480
  97.7 0.0 copy-start.2
  97.7 0.0 copy-start.1
  97.7 1.0 slice.3
  98.7 0.0 copy-start
  98.7 3.1 %bitcast_multiply_fusion = f32[768,768]{1,0:T(8,128)} fusion(s16[768,768]{1,0:T(8,128)(2,1)} %get-tuple-element.10, f32[4,768]{1,0:T(4,128)S(1)} %bitcast.9), kind=kLoop, calls=%fused_computation | loop fusion | flops 1179648 | bytes 3551232 | tf_op jit(solution)/shard_map/mul | solution.py:531
  101.8 0.0 copy-done.2
  101.8 0.6 copy.16
  102.4 0.0 copy-done.1
  102.4 0.8 copy.17
  103.2 0.0 copy-done
  103.2 0.8 copy.18
  (1 shorter events, 0.0 us)
Async XLA Ops:
  97.7 4.1 %copy-start.2 = (f32[6,128]{1,0:T(8,128)S(1)}, f32[6,128]{1,0:T(8,128)}, u32[]{:S(2)}) copy-start(f32[6,128]{1,0:T(8,128)} %get-tuple-element.9) | copy-start | bytes 9220
  97.7 4.7 %copy-start.1 = (f32[192,768]{1,0:T(8,128)S(1)}, f32[192,768]{1,0:T(8,128)}, u32[]{:S(2)}) copy-start(f32[192,768]{1,0:T(8,128)} %get-tuple-element.20) | copy-start | bytes 1769476
  98.7 4.5 %copy-start = (f32[192,768]{1,0:T(8,128)S(1)}, f32[192,768]{1,0:T(8,128)}, u32[]{:S(2)}) copy-start(f32[192,768]{1,0:T(8,128)} %get-tuple-element.21) | copy-start | bytes 1769476
